TPU v7x, 256 devices: a whole 4x4x8 slice. The times are simulated.
256 devices in a mesh: tmpl: 8 (over z), chan: 16 (over x_hi, y, core), tm: 2 (over x_lo).
Axes of the slice: x: 4 (x_hi: 2, x_lo: 2; x = x_hi * 2 + x_lo), y: 4, z: 8, core: 2. Of those that a mesh axis runs over, the one named last changes fastest.
Arguments:
- raw: bfloat16 [1024, 8192], P('chan', ('tmpl', 'tm')), may hold values from -6 to 6
- dead_mask: int32 [1024], P('chan'), may hold values 0 or 1
- templates: bfloat16 [32, 1024, 512], P('tmpl', 'chan'), may hold values from -0.0078125 to 0.0078125
- assign: int32 [32], P('tmpl'), may hold values from 0 to 31, as said below
- w_enc: bfloat16 [16, 1, 3, 3], replicated, may hold values from -2 to 2
- b_enc: float32 [16], replicated, may hold values from -3 to 3
- w_mid: bfloat16 [32, 16, 3, 3], replicated, may hold values from -0.5 to 0.5
- b_mid: float32 [32], replicated, may hold values from -3 to 3
- w_dec: bfloat16 [16, 48, 3, 3], replicated, may hold values from -0.3125 to 0.3125
- b_dec: float32 [16], replicated, may hold values from -3 to 3
- w_out: bfloat16 [16], replicated, may hold values from -1.5 to 1.5
- b_out: float32 [1], replicated, may hold values from -3 to 3
Outputs:
- denoised: bfloat16 [1024, 8192], P('chan', ('tmpl', 'tm'))
- corr: float32 [32, 8, 2, 512], P('tmpl', None, 'tm', 'chan')
Inputs may be any that keep to these rules, and one draw needn't show every extreme that they name: `assign`: for each j, entries 4 * j to 4 * j + 3 hold exactly those numbers in some order.
All inputs are finite; a program needn't handle non-finite values. No bound on the sum of `dead_mask` on one device may be relied on, other than what follows from the above.
Results may differ from a plain program's by a relative error of at most 0.018.
Values may be sent and summed in bfloat16 or wider, within the bound.
A program may use at most 128 MiB of HBM per device.

v0:
```python
import math

import jax
import jax.numpy as jnp
from jax import lax
from jax.sharding import PartitionSpec as P


def extended(cells, sides, width):
    for axis, dim in sides:
        count = lax.axis_size(axis)
        ends = count - 1
        head = lax.slice_in_dim(cells, 0, width, axis=dim)
        tail = lax.slice_in_dim(cells, cells.shape[dim] - width, cells.shape[dim], axis=dim)
        cells = jnp.concatenate(
            [
                lax.ppermute(tail, axis, [(i, (i + 1) % count) for i in range(ends)]),
                cells,
                lax.ppermute(head, axis, [((i + 1) % count, i) for i in range(ends)]),
            ],
            axis=dim,
        )
    return cells


def swapped(x, axis, apart):
    return lax.ppermute(x, axis, [(i, i ^ 1 << apart) for i in range(lax.axis_size(axis))])


def forward_table(patch_len):
    sample_ids = jnp.arange(patch_len, dtype=jnp.int32)[:, None]
    freq_ids = jnp.arange(2 * patch_len, dtype=jnp.int32)[None, :]
    phase = (sample_ids * freq_ids % (2 * patch_len)).astype(jnp.float32) * (math.pi / patch_len)
    return jnp.concatenate([jnp.cos(phase), -jnp.sin(phase)], axis=1).astype(jnp.bfloat16)


def inverse_table(patch_len):
    freq_ids = jnp.arange(2 * patch_len, dtype=jnp.int32)[:, None]
    lag_ids = jnp.arange(patch_len, dtype=jnp.int32)[None, :]
    phase = (freq_ids * lag_ids % (2 * patch_len)).astype(jnp.float32) * (math.pi / patch_len)
    return jnp.concatenate([jnp.cos(phase), -jnp.sin(phase)], axis=0) / (2.0 * patch_len)


def alternate_signs(patch_len):
    single = jnp.where(jnp.arange(2 * patch_len) % 2 == 0, 1.0, -1.0).astype(jnp.float32)
    return jnp.concatenate([single, single])


def convolve(picture, weight, bias_term):
    padded = extended(picture, (("chan", 2),), 1)
    result = lax.conv_general_dilated(
        padded,
        weight,
        (1, 1),
        ((0, 0), (1, 1)),
        dimension_numbers=("NCHW", "OIHW", "NCHW"),
        preferred_element_type=jnp.float32,
    )
    return jax.nn.relu(result + bias_term[None, :, None, None]).astype(jnp.bfloat16)


def cross_products(spectrum, tspectrum, half_len):
    spec_re = spectrum[..., :half_len]
    spec_im = spectrum[..., half_len:]
    tmpl_re = tspectrum[..., :half_len]
    tmpl_im = tspectrum[..., half_len:]
    f32 = jnp.float32
    real_part = jnp.einsum(
        "bcf,kcf->kbf", spec_re, tmpl_re, preferred_element_type=f32
    ) + jnp.einsum("bcf,kcf->kbf", spec_im, tmpl_im, preferred_element_type=f32)
    imag_part = jnp.einsum(
        "bcf,kcf->kbf", spec_im, tmpl_re, preferred_element_type=f32
    ) - jnp.einsum("bcf,kcf->kbf", spec_re, tmpl_im, preferred_element_type=f32)
    return jnp.concatenate([real_part, imag_part], axis=-1)


def body(raw, dead_mask, templates, assign, w_enc, b_enc, w_mid, b_mid, w_dec, b_dec, w_out, b_out):
    rows_here, patch_len = raw.shape
    feature_maps = w_enc.shape[0]
    alive = dead_mask.astype(jnp.float32)
    cleaned = raw * alive[:, None].astype(jnp.bfloat16)
    encoded = convolve(cleaned[None, None], w_enc, b_enc)
    pooled = (
        encoded.astype(jnp.float32)
        .reshape(1, feature_maps, rows_here // 2, 2, patch_len // 2, 2)
        .mean(axis=(3, 5))
        .astype(jnp.bfloat16)
    )
    middle = convolve(pooled, w_mid, b_mid)
    upsampled = jnp.repeat(jnp.repeat(middle, 2, axis=2), 2, axis=3)
    merged = jnp.concatenate([upsampled, encoded], axis=1)
    decoded = convolve(merged, w_dec, b_dec)
    branch = jnp.einsum("g,gct->ct", w_out, decoded[0], preferred_element_type=jnp.float32)
    denoised = (alive[:, None] * (cleaned.astype(jnp.float32) + branch + b_out[0])).astype(
        jnp.bfloat16
    )
    forward = forward_table(patch_len)
    own_spectrum = jnp.dot(denoised, forward, preferred_element_type=jnp.float32).astype(
        jnp.bfloat16
    )
    gathered = lax.all_gather(own_spectrum[None], "tmpl", axis=0, tiled=True)
    tspectra = jnp.einsum(
        "kct,tf->kcf", templates, forward, preferred_element_type=jnp.float32
    ).astype(jnp.bfloat16)
    half_len = 2 * patch_len
    parity = lax.axis_index("tm")
    signs = alternate_signs(patch_len)
    partner = swapped(gathered, "tm", 0)
    shifted = jnp.concatenate([partner[1:], jnp.zeros_like(partner[:1])], axis=0)
    following = jnp.where(parity == 0, partner, shifted)
    combined = cross_products(gathered, tspectra, half_len) + signs * cross_products(
        following, tspectra, half_len
    )
    tmpl_here, blocks_here = (combined.shape[0], combined.shape[1])
    lagged = jnp.dot(
        combined.reshape(-1, 2 * half_len),
        inverse_table(patch_len),
        precision=lax.Precision.HIGHEST,
    ).reshape(tmpl_here, blocks_here, patch_len)
    local_rows = assign % tmpl_here
    selector = (local_rows[:, None] == jnp.arange(tmpl_here, dtype=jnp.int32)[None, :]).astype(
        jnp.float32
    )
    ordered = jnp.einsum("rk,kbj->rbj", selector, lagged, precision=lax.Precision.HIGHEST)
    summed = lax.psum(ordered.astype(jnp.bfloat16), "chan").astype(jnp.float32)
    share_width = patch_len // lax.axis_size("chan")
    lag_piece = lax.dynamic_slice_in_dim(
        summed, lax.axis_index("chan") * share_width, share_width, 2
    )
    return (denoised, lag_piece[:, :, None, :])


def solution(mesh):
    return jax.shard_map(
        body,
        mesh=mesh,
        in_specs=(
            P("chan", ("tmpl", "tm")),
            P("chan"),
            P("tmpl", "chan", None),
            P("tmpl"),
            P(),
            P(),
            P(),
            P(),
            P(),
            P(),
            P(),
            P(),
        ),
        out_specs=(P("chan", ("tmpl", "tm")), P("tmpl", None, "tm", "chan")),
        check_vma=False,
    )
```

profile of v0, /device:TPU:4, one launch (start us, length us, event | category | flops | bytes accessed | tf_op | source)
XLA Modules:
  0.0 430.1 jit_solution(6242135016858896554)
XLA Ops:
  11.3 7.3 %collective-permute-start.1 = (bf16[1,1,1,512]{3,2,1,0:T(2,128)(2,1)S(1)}, bf16[1,1,1,512]{3,2,1,0:T(2,128)(2,1)S(1)}, u32[]{:S(2)}, u32[]{:S(2)}) collective-permute-start(bf16[1,1,1,512]{3,2,1,0:T(2,128)(2,1)S(1)} %get-tuple-element.23), channel_id=1, source_target_pairs={{2,0},{4,2},{6,4},{8,6},{10,8},{12,10},{14,12},{16,14},{18,16},{20... | collective-permute-start | bytes 3080 | tf_op jit(solution)/shard_map/ppermute | solution.py:19
  22.0 13.8 %maximum_convert_fusion.1 = bf16[64,8,65,16]{3,1,2,0:T(8,128)(2,1)} fusion(bf16[1,66,8,67]{2,0,3,1:T(2,128)(2,1)S(1)} %copy.136, f32[16]{0:T(128)S(1)} %copy-done.19, pred[8,65]{0,1:T(8,128)(4,1)S(1)} %copy-done.24, bf16[16,1,3,3]{0,3,2,1:T(4,128)(2,1)S(1)} %copy-done.18), kind=kOutput, calls=%fused_computation.3 | convolution fusion | flops 11714560 | bytes 1136584 | tf_op jit(solution)/shard_map/conv_general_dilated | solution.py:51
  35.8 8.2 %copy.138 = bf16[64,8,65,16]{2,1,3,0:T(8,128)(2,1)S(1)} copy(bf16[64,8,65,16]{3,1,2,0:T(8,128)(2,1)} %maximum_convert_fusion.1) | data formatting | bytes 2129920 | tf_op jit(solution)/shard_map/convert_element_type | solution.py:59
  44.0 2.5 reshape.77
  48.1 8.7 %copy.139 = f32[1,16,64,512]{1,3,2,0:T(8,128)} copy(f32[1,16,64,512]{3,1,2,0:T(8,128)S(1)} %get-tuple-element.18) | data formatting | bytes 4194304 | tf_op jit(solution)/shard_map/reshape | solution.py:85
  56.8 17.1 %reduce_sum.9 = f32[16,32,256]{0,2,1:T(8,128)} reduce(f32[16,32,2,256,2]{0,4,3,2,1:T(2,128)} %bitcast.107, f32[]{:T(128)} %constant.70.clone.1), dimensions={2,4}, to_apply=%region_0.1 | reduce | flops 393216 | bytes 2621444 | tf_op jit(solution)/shard_map/reduce_sum | solution.py:86
  73.9 2.7 fusion.28
  79.2 7.4 %collective-permute-start.3 = (bf16[1,16,1,256]{1,3,2,0:T(8,128)(2,1)}, bf16[1,16,1,256]{1,3,2,0:T(8,128)(2,1)S(1)}, u32[]{:S(2)}, u32[]{:S(2)}) collective-permute-start(bf16[1,16,1,256]{1,3,2,0:T(8,128)(2,1)} %get-tuple-element.17), channel_id=1, source_target_pairs={{2,0},{4,2},{6,4},{8,6},{10,8},{12,10},{14,12},{16,14},{18,16},{20... | collective-permute-start | bytes 24584 | tf_op jit(solution)/shard_map/ppermute | solution.py:19
  88.1 2.7 copy.147
  92.9 2.1 reshape.80
  95.0 3.5 copy.144
  99.4 6.1 %maximum_convert_fusion.2 = bf16[32,8,33,32]{3,1,2,0:T(8,128)(2,1)} fusion(f32[32]{0:T(128)S(1)} %copy-done.20, pred[8,33]{0,1:T(8,128)(4,1)S(1)} %copy-done.26, bf16[32,16,3,3]{0,1,3,2:T(8,128)(2,1)S(1)} %copy-done.16, bf16[16,34,1,7,2]{0,3,4,1,2:T(8,128)(2,1)S(1)} %slice.66, bf16[16,34,1,8,33]{0,3,4,1,2:T(8,128)(2,1)} %copy.144), kind=kOutput, calls=%fused_computation.15 | convolution fusion | flops 79852032 | bytes 852744 | tf_op jit(solution)/shard_map/conv_general_dilated | solution.py:51
  105.6 4.7 %copy.145 = bf16[32,8,33,32]{2,1,3,0:T(8,128)(2,1)} copy(bf16[32,8,33,32]{3,1,2,0:T(8,128)(2,1)} %maximum_convert_fusion.2) | data formatting | bytes 1081344 | tf_op jit(solution)/shard_map/convert_element_type | solution.py:59
  110.3 3.2 reshape.84
  113.7 4.4 %copy.146 = bf16[32,64,256]{1,0,2:T(8,128)(2,1)} copy(bf16[32,64,256]{2,0,1:T(8,128)(2,1)S(1)} %bitcast.111) | data formatting | bytes 2097152 | tf_op jit(solution)/shard_map/broadcast_in_dim | solution.py:90
  118.1 2.2 broadcast_in_dim.43
  120.4 6.9 %slice_maximum_fusion = (bf16[1,48,1,512]{2,1,3,0:T(8,128)(2,1)}, bf16[1,48,1,512]{2,1,3,0:T(8,128)(2,1)}) fusion(bf16[1,16,64,512]{2,1,3,0:T(8,128)(2,1)S(1)} %copy.147, bf16[1,32,64,512]{2,1,3,0:T(8,128)(2,1)S(1)} %bitcast.108), kind=kLoop, calls=%fused_computation.10 | loop fusion | flops 196608 | bytes 3244032 | tf_op jit(solution)/shard_map/concatenate | solution.py:91
  127.2 7.2 %copy.148 = bf16[1,48,1,512]{3,1,2,0:T(8,128)(2,1)S(1)} copy(bf16[1,48,1,512]{2,1,3,0:T(8,128)(2,1)} %get-tuple-element.12) | data formatting | bytes 98304 | tf_op jit(solution)/shard_map/slice | solution.py:14
  136.4 6.9 %copy.149 = bf16[1,48,1,512]{3,1,2,0:T(8,128)(2,1)S(1)} copy(bf16[1,48,1,512]{2,1,3,0:T(8,128)(2,1)} %get-tuple-element.13) | data formatting | bytes 98304 | tf_op jit(solution)/shard_map/slice | solution.py:13
  143.3 7.3 %collective-permute-start.5 = (bf16[1,48,1,512]{3,1,2,0:T(8,128)(2,1)S(1)}, bf16[1,48,1,512]{3,1,2,0:T(8,128)(2,1)}, u32[]{:S(2)}, u32[]{:S(2)}) collective-permute-start(bf16[1,48,1,512]{3,1,2,0:T(8,128)(2,1)S(1)} %copy.149), channel_id=1, source_target_pairs={{2,0},{4,2},{6,4},{8,6},{10,8},{12,10},{14,12},{16,14},{18,16},{20... | collective-permute-start | bytes 147464 | tf_op jit(solution)/shard_map/ppermute | solution.py:19
  150.5 9.2 %negate_convert_fusion = (bf16[512,1024]{1,0:T(8,128)(2,1)S(1)}, bf16[512,1024]{1,0:T(8,128)(2,1)}) fusion(), kind=kLoop, calls=%fused_computation.55 | loop fusion | flops 8912896 | bytes 2097152 | tf_op jit(solution)/shard_map/convert.2
  160.4 7.0 %copy.150 = bf16[1,48,1,512]{2,1,3,0:T(8,128)(2,1)} copy(bf16[1,48,1,512]{3,1,2,0:T(8,128)(2,1)S(1)} %collective-permute-done.4) | data formatting | bytes 98304 | tf_op jit(solution)/shard_map/ppermute | solution.py:17
  167.4 7.7 %copy.151 = bf16[1,48,1,512]{2,1,3,0:T(8,128)(2,1)} copy(bf16[1,48,1,512]{3,1,2,0:T(8,128)(2,1)} %collective-permute-done.5) | data formatting | bytes 98304 | tf_op jit(solution)/shard_map/ppermute | solution.py:19
  175.1 9.6 %maximum_bitcast_fusion = bf16[48,66,1,512]{1,0,3,2:T(8,128)(2,1)S(1)} fusion(bf16[1,48,1,512]{2,1,3,0:T(8,128)(2,1)} %copy.151, bf16[1,16,64,512]{2,1,3,0:T(8,128)(2,1)S(1)} %copy.147, bf16[1,32,64,512]{2,1,3,0:T(8,128)(2,1)} %bitcast.109, bf16[1,48,1,512]{2,1,3,0:T(8,128)(2,1)} %copy.150), kind=kLoop, calls=%fused_computation.11 | loop fusion | flops 12976128 | bytes 6488064 | tf_op jit(solution)/shard_map/concatenate | solution.py:15
  184.7 3.9 pad.5
  188.6 12.6 %copy.154 = bf16[48,66,1,8,65]{0,3,4,1,2:T(8,128)(2,1)} copy(bf16[48,66,1,8,65]{1,0,4,3,2:T(8,128)(2,1)} %bitcast.110) | data formatting | bytes 6589440 | tf_op jit(solution)/shard_map/conv_general_dilated | solution.py:51
  202.3 23.2 %maximum_convert_fusion = bf16[64,8,65,16]{3,1,2,0:T(8,128)(2,1)} fusion(bf16[16,48,3,3]{1,0,3,2:T(8,128)(2,1)S(1)} %copy-done.17, bf16[48,66,1,7,2]{0,3,4,1,2:T(8,128)(2,1)S(1)} %slice.70, bf16[48,66,1,8,65]{0,3,4,1,2:T(8,128)(2,1)} %copy.154, f32[16]{0:T(128)S(1)} %copy-done.21, pred[8,65]{0,1:T(8,128)(4,1)S(1)} %copy-done.25), kind=kOutput, calls=%fused_computation.2 | convolution fusion | flops 472380928 | bytes 4462792 | tf_op jit(solution)/shard_map/conv_general_dilated | solution.py:51
  225.6 8.3 %copy.155 = bf16[64,8,65,16]{2,1,3,0:T(8,128)(2,1)S(1)} copy(bf16[64,8,65,16]{3,1,2,0:T(8,128)(2,1)} %maximum_convert_fusion) | data formatting | bytes 2129920 | tf_op jit(solution)/shard_map/convert_element_type | solution.py:59
  234.0 2.5 reshape.91
  238.2 2.5 convolution_convert_fusion.1
  241.6 40.7 %all-gather.3.cloned.1.call-done = bf16[512,2048]{1,0:T(8,128)(2,1)} async-done(((bf16[64,2048]{1,0:T(8,128)(2,1)}), bf16[512,2048]{1,0:T(8,128)(2,1)}) %all-gather.3.cloned.1.call-update) | async-done | bytes 2097168 | tf_op jit(solution)/shard_map/all_gather | solution.py:101
  284.9 9.2 %sine_negate_fusion = (f32[1024,512]{1,0:T(8,128)}, f32[1024,512]{1,0:T(8,128)}) fusion(), kind=kLoop, calls=%fused_computation.48 | loop fusion | flops 7864320 | bytes 4194304 | tf_op jit(solution)/shard_map/neg | solution.py:41
  295.3 3.5 copy.181
  298.8 2.5 copy.182
  301.3 3.0 fusion.93
  304.3 2.6 add_bitcast_fusion.1
  308.7 3.0 fusion.94
  311.7 2.6 subtract_bitcast_fusion.1
  314.3 2.5 copy.163
  316.8 9.4 %collective-permute-done.6 = bf16[8,64,2048]{2,1,0:T(8,128)(2,1)} collective-permute-done((bf16[8,64,2048]{2,1,0:T(8,128)(2,1)}, bf16[8,64,2048]{2,1,0:T(8,128)(2,1)}, u32[]{:S(2)}, u32[]{:S(2)}) %collective-permute-start.6) | collective-permute-done | bytes 2097184 | tf_op jit(solution)/shard_map/ppermute | solution.py:27
  326.2 5.7 %copy.165 = bf16[8,64,2048]{1,0,2:T(8,128)(2,1)} copy(bf16[8,64,2048]{2,1,0:T(8,128)(2,1)} %collective-permute-done.6) | data formatting | bytes 4194304 | tf_op jit(solution)/shard_map/ppermute | solution.py:27
  331.9 2.9 slice.76
  338.5 2.7 fusion.41
  341.2 2.6 add_bitcast_fusion
  343.8 2.6 copy.170
  346.5 4.2 subtract_bitcast_fusion
  352.9 4.2 fusion.10
  357.4 65.0 %psum.7 = bf16[4,8,512]{2,0,1:T(4,128)(2,1)S(1)} all-reduce(bf16[4,8,512]{2,0,1:T(4,128)(2,1)S(1)} %convolution_convert_fusion.2), channel_id=1, replica_groups=mesh['tmpl'=8,'chan'=16,'tm'=2] {'chan'}, use_global_device_ids=true, to_apply=%region_1.2 | all-reduce | flops 16384 | bytes 65536 | tf_op jit(solution)/shard_map/psum | solution.py:125
  (103 shorter events, 34.2 us)
Async XLA Ops:
  7.2 233.6 %copy-start = (bf16[4,64,512]{2,1,0:T(8,128)(2,1)S(1)}, bf16[4,64,512]{2,1,0:T(8,128)(2,1)}, u32[]{:S(2)}) copy-start(bf16[4,64,512]{2,1,0:T(8,128)(2,1)} %param.14) | copy-start | bytes 786436
  7.2 14.8 %copy-start.24 = (pred[8,65]{0,1:T(8,128)(4,1)S(1)}, pred[8,65]{0,1:T(8,128)(4,1)}, u32[]{:S(2)}) copy-start(pred[8,65]{0,1:T(8,128)(4,1)} %constant.104) | copy-start | bytes 1564
  7.2 14.8 %copy-start.18 = (bf16[16,1,3,3]{0,3,2,1:T(4,128)(2,1)S(1)}, bf16[16,1,3,3]{0,3,2,1:T(4,128)(2,1)}, u32[]{:S(2)}) copy-start(bf16[16,1,3,3]{0,3,2,1:T(4,128)(2,1)} %param.16) | copy-start | bytes 868
  7.2 14.8 %copy-start.19 = (f32[16]{0:T(128)S(1)}, f32[16]{0:T(128)}, u32[]{:S(2)}) copy-start(f32[16]{0:T(128)} %param.17) | copy-start | bytes 196
  7.2 275.1 %all-gather.3.cloned.1.call-start = ((), (), s32[]{:S(2)}) async-start(), calls=%async_computation | async-start | bytes 2359296 | tf_op jit(solution)/shard_map/all_gather | solution.py:101
  8.5 10.1 %copy-start.13 = (bf16[64]{0:T(256)(128)(2,1)}, bf16[64]{0:T(256)(128)(2,1)S(1)}, u32[]{:S(2)}) copy-start(bf16[64]{0:T(256)(128)(2,1)S(1)} %get-tuple-element.25) | copy-start | bytes 388
  9.4 9.2 %collective-permute-start = (bf16[1,1,1,512]{3,2,1,0:T(2,128)(2,1)S(1)}, bf16[1,1,1,512]{3,2,1,0:T(2,128)(2,1)S(1)}, u32[]{:S(2)}, u32[]{:S(2)}) collective-permute-start(bf16[1,1,1,512]{3,2,1,0:T(2,128)(2,1)S(1)} %get-tuple-element.22), channel_id=1, source_target_pairs={{0,2},{2,4},{4,6},{6,8},{8,10},{10,12},{12,14},{14,16},{16,18},{18... | collective-permute-start | bytes 3080 | tf_op jit(solution)/shard_map/ppermute | solution.py:17
  11.3 8.6 %collective-permute-start.1 = (bf16[1,1,1,512]{3,2,1,0:T(2,128)(2,1)S(1)}, bf16[1,1,1,512]{3,2,1,0:T(2,128)(2,1)S(1)}, u32[]{:S(2)}, u32[]{:S(2)}) collective-permute-start(bf16[1,1,1,512]{3,2,1,0:T(2,128)(2,1)S(1)} %get-tuple-element.23), channel_id=1, source_target_pairs={{2,0},{4,2},{6,4},{8,6},{10,8},{12,10},{14,12},{16,14},{18,16},{20... | collective-permute-start | bytes 3080 | tf_op jit(solution)/shard_map/ppermute | solution.py:19
  77.3 13.5 %collective-permute-start.2 = (bf16[1,16,1,256]{1,3,2,0:T(8,128)(2,1)}, bf16[1,16,1,256]{1,3,2,0:T(8,128)(2,1)S(1)}, u32[]{:S(2)}, u32[]{:S(2)}) collective-permute-start(bf16[1,16,1,256]{1,3,2,0:T(8,128)(2,1)} %get-tuple-element.16), channel_id=1, source_target_pairs={{0,2},{2,4},{4,6},{6,8},{8,10},{10,12},{12,14},{14,16},{16,18},{18... | collective-permute-start | bytes 24584 | tf_op jit(solution)/shard_map/ppermute | solution.py:17
  79.2 11.6 %collective-permute-start.3 = (bf16[1,16,1,256]{1,3,2,0:T(8,128)(2,1)}, bf16[1,16,1,256]{1,3,2,0:T(8,128)(2,1)S(1)}, u32[]{:S(2)}, u32[]{:S(2)}) collective-permute-start(bf16[1,16,1,256]{1,3,2,0:T(8,128)(2,1)} %get-tuple-element.17), channel_id=1, source_target_pairs={{2,0},{4,2},{6,4},{8,6},{10,8},{12,10},{14,12},{16,14},{18,16},{20... | collective-permute-start | bytes 24584 | tf_op jit(solution)/shard_map/ppermute | solution.py:19
  92.9 6.5 %copy-start.16 = (bf16[32,16,3,3]{0,1,3,2:T(8,128)(2,1)S(1)}, bf16[32,16,3,3]{0,1,3,2:T(8,128)(2,1)}, u32[]{:S(2)}) copy-start(bf16[32,16,3,3]{0,1,3,2:T(8,128)(2,1)} %param.18) | copy-start | bytes 27652
  92.9 6.5 %copy-start.20 = (f32[32]{0:T(128)S(1)}, f32[32]{0:T(128)}, u32[]{:S(2)}) copy-start(f32[32]{0:T(128)} %param.19) | copy-start | bytes 388
  92.9 6.5 %copy-start.26 = (pred[8,33]{0,1:T(8,128)(4,1)S(1)}, pred[8,33]{0,1:T(8,128)(4,1)}, u32[]{:S(2)}) copy-start(pred[8,33]{0,1:T(8,128)(4,1)} %constant.105) | copy-start | bytes 796
  120.3 6.9 %copy-start.3 = (bf16[32,64,256,2]{1,0,3,2:T(8,128)(2,1)}, bf16[32,64,256,2]{1,0,3,2:T(8,128)(2,1)S(1)}, u32[]{:S(2)}) copy-start(bf16[32,64,256,2]{1,0,3,2:T(8,128)(2,1)S(1)} %broadcast_in_dim.43) | copy-start | bytes 6291460
  134.5 25.9 %collective-permute-start.4 = (bf16[1,48,1,512]{3,1,2,0:T(8,128)(2,1)S(1)}, bf16[1,48,1,512]{3,1,2,0:T(8,128)(2,1)S(1)}, u32[]{:S(2)}, u32[]{:S(2)}) collective-permute-start(bf16[1,48,1,512]{3,1,2,0:T(8,128)(2,1)S(1)} %copy.148), channel_id=1, source_target_pairs={{0,2},{2,4},{4,6},{6,8},{8,10},{10,12},{12,14},{14,16},{16,18},{18... | collective-permute-start | bytes 147464 | tf_op jit(solution)/shard_map/ppermute | solution.py:17
  143.3 24.1 %collective-permute-start.5 = (bf16[1,48,1,512]{3,1,2,0:T(8,128)(2,1)S(1)}, bf16[1,48,1,512]{3,1,2,0:T(8,128)(2,1)}, u32[]{:S(2)}, u32[]{:S(2)}) collective-permute-start(bf16[1,48,1,512]{3,1,2,0:T(8,128)(2,1)S(1)} %copy.149), channel_id=1, source_target_pairs={{2,0},{4,2},{6,4},{8,6},{10,8},{12,10},{14,12},{16,14},{18,16},{20... | collective-permute-start | bytes 147464 | tf_op jit(solution)/shard_map/ppermute | solution.py:19
  188.6 13.7 %copy-start.17 = (bf16[16,48,3,3]{1,0,3,2:T(8,128)(2,1)S(1)}, bf16[16,48,3,3]{1,0,3,2:T(8,128)(2,1)}, u32[]{:S(2)}) copy-start(bf16[16,48,3,3]{1,0,3,2:T(8,128)(2,1)} %param.20) | copy-start | bytes 41476
  188.6 13.7 %copy-start.21 = (f32[16]{0:T(128)S(1)}, f32[16]{0:T(128)}, u32[]{:S(2)}) copy-start(f32[16]{0:T(128)} %param.21) | copy-start | bytes 196
  188.6 13.7 %copy-start.25 = (pred[8,65]{0,1:T(8,128)(4,1)S(1)}, pred[8,65]{0,1:T(8,128)(4,1)}, u32[]{:S(2)}) copy-start(pred[8,65]{0,1:T(8,128)(4,1)} %constant.104) | copy-start | bytes 1564
  233.9 2.6 copy-start.22
  233.9 4.1 copy-start.11
  233.9 4.1 copy-start.14
  233.9 4.1 copy-start.15
  238.0 2.7 copy-start.23
  238.0 2.7 copy-start.9
  238.1 2.6 copy-start.12
  282.3 44.0 %collective-permute-start.6 = (bf16[8,64,2048]{2,1,0:T(8,128)(2,1)}, bf16[8,64,2048]{2,1,0:T(8,128)(2,1)}, u32[]{:S(2)}, u32[]{:S(2)}) collective-permute-start(bf16[8,64,2048]{2,1,0:T(8,128)(2,1)} %bitcast.112), channel_id=1, source_target_pairs={{0,1},{1,0},{2,3},{3,2},{4,5},{5,4},{6,7},{7,6},{8,9},{9,8},{10,11... | collective-permute-start | bytes 6291464 | tf_op jit(solution)/shard_map/ppermute | solution.py:27
  284.9 9.3 %copy-start.8 = (bf16[512,2048]{1,0:T(8,128)(2,1)S(1)}, bf16[512,2048]{1,0:T(8,128)(2,1)}, u32[]{:S(2)}) copy-start(bf16[512,2048]{1,0:T(8,128)(2,1)} %all-gather.3.cloned.1.call-done) | copy-start | bytes 6291460
  301.3 3.0 copy-start.5
  308.7 3.0 copy-start.4
  331.9 3.4 copy-start.2
  337.2 4.0 copy-start.1
  343.8 2.6 copy-start.6
  350.7 2.2 copy-start.7
  350.7 2.2 copy-start.10
Sparse Core Ops, SparseCore 0:
  240.8 41.4 all-gather.2
where the time goes:
time: 437 us; the launch traced here: 430 us
  local copies, waits for them, and re-layouts  134 us (31%)
  matrix products  74.2 us (17%)
  blocking collectives  65 us (15%)
  other arithmetic  61.5 us (14%)
  waiting for transfers between devices  51.4 us (12%)
  starting transfers between devices  28.9 us (7%)
  between operations  15.6 us (4%)
    psum x1, blocking collectives, body(): summed = lax.psum(ordered.astype(jnp.bfloat16), 'chan').astype(jnp.float32)  65 us
    conv_general_dilated x3, matrix products, convolve(): lax.conv_general_dilated(padded, weight, (1, 1), ((0, 0), (1, 1)), dimens...  43.1 us
    all_gather x1, waiting for transfers between devices, body(): gathered = lax.all_gather(own_spectrum[None], 'tmpl', axis=0, tiled=True)  40.7 us
    convert_element_type x8, local copies, waits for them, and re-layouts, convolve(): jax.nn.relu(result + bias_term[None, :, None, None]).astype(jnp.bfloat16)  32.2 us
    conv_general_dilated x8, local copies, waits for them, and re-layouts, convolve(): lax.conv_general_dilated(padded, weight, (1, 1), ((0, 0), (1, 1)), dimens...  22 us
    ppermute x3, starting transfers between devices, extended(): lax.ppermute(head, axis, [((i + 1) % count, i) for i in range(ends)])  21.9 us
    reduce_sum x1, other arithmetic, body(): pooled = encoded.astype(jnp.float32).reshape(1, feature_maps, rows_here /...  17.1 us
    concatenate x3, other arithmetic, extended(): jnp.concatenate([lax.ppermute(tail, axis, [(i, (i + 1) % count) for i in...  10.6 us
  transfers between devices with their start and end apart: 8, of which 3 were waited for; matrix products, arithmetic and copies ran while one was open for 14% of the time, Pallas kernels for 0%

commit v1 on v0

v1 whole, which is shorter than its diff:
```python
import functools
import math

import jax
import jax.numpy as jnp
import numpy as np
from jax import lax
from jax.experimental import pallas as pl
from jax.experimental.pallas import tpu as pltpu
from jax.sharding import PartitionSpec as P

BF = jnp.bfloat16
F32 = jnp.float32
MESH = pl.DeviceIdType.MESH
ROWS = 64
TL = 512
HALF = 256
NZ = 8
NC = 16
BIG = -1e30


def middle_table():
    q = np.zeros((16, 3, 3, 512), np.float32)
    for g in range(16):
        for rr in range(3):
            for v in range(3):
                q[g, rr, v, rr * 48 + v * 16 + g] = 1
    return q.reshape(144, 512)


def encoder_table():
    q = np.zeros((4, 3, 3, 128), np.float32)
    for v in range(4):
        for rr in range(3):
            for dt in range(3):
                q[v, rr, dt, rr * 8 + v + dt] = 1
    return q.reshape(4, 9, 128)


def decoder_table():
    q = np.zeros((4, 48, 3, 3, 640), np.float32)
    for ps in range(2):
        for pr in range(2):
            n = ps * 2 + pr
            for rr in range(4):
                for v in range(4):
                    if 0 <= rr - pr <= 2 and 0 <= v - ps <= 2:
                        for g in range(16):
                            q[n, 32 + g, rr - pr, v - ps, rr * 64 + v * 16 + g] = 1
            for dr in range(3):
                for dt in range(3):
                    rr = (pr + dr - 1) // 2 + 1
                    v = (ps + dt - 1) // 2 + 1
                    for m in range(32):
                        q[n, m, dr, dt, 256 + rr * 96 + v * 32 + m] = 1
    return q.reshape(4, 432, 640)


def spectrum_table():
    s = np.arange(TL)[:, None]
    f = np.arange(TL)[None, :]
    phase = ((s * f) % (2 * TL)) * (math.pi / TL)
    re = np.cos(phase)
    im = -np.sin(phase)
    im[:, 0] = np.where(np.arange(TL) % 2 == 0, 1.0, -1.0)
    return np.concatenate([re, im], axis=1).astype(np.float32)


def lag_table():
    f = np.arange(TL)[:, None]
    j = np.arange(TL)[None, :]
    phase = ((f * j) % (2 * TL)) * (math.pi / TL)
    re = np.cos(phase) * 2
    im = -np.sin(phase) * 2
    re[0] = 1
    im[0] = np.where(np.arange(TL) % 2 == 0, 1.0, -1.0)
    full = (np.concatenate([re, im], axis=0) / (2 * TL)).astype(np.float32)
    hi = full.astype(BF)
    lo = (full - hi.astype(np.float32)).astype(BF)
    return hi, lo


def iota(shape, dim):
    return lax.broadcasted_iota(jnp.int32, shape, dim)


def mm(a, b):
    return jnp.dot(a, b, preferred_element_type=F32)


def column(ref, count, lanes):
    rows = iota((count, lanes), 0)
    out = jnp.zeros((count, lanes), F32)
    for g in range(count):
        out = jnp.where(rows == g, ref[g], out)
    return out


def kernel(
    raw_ref, mask_ref, tmpl_ref, assign_ref, wenc_ref, benc_ref, wmid_ref, bmid_ref,
    wdec_ref, bdec_ref, wout_ref, bout_ref, q1_ref, q2_ref, q3_ref, f_hbm, ih_hbm, il_hbm,
    den_ref, corr_ref,
    f_ref, ih_ref, il_ref, clean_ref, halo_ref, cv_ref, w1_ref, w2_ref, w3s_ref, w3m_ref,
    ev_ref, pv_ref, mv_ref, dp_ref, own_ref, alive_ref, b2_ref, b3_ref, tg_ref, ts_ref, sd_ref, xw_ref,
    z_ref, g_ref, lag_ref, rs_ref, rr_ref, as_ref, ar_ref,
    tab_sem, halo_send, halo_recv, ring_send, ring_recv, x_send, x_recv,
    rs_send, rs_recv, a_send, a_recv,
):
    z = lax.axis_index("tmpl")
    c = lax.axis_index("chan")
    p = lax.axis_index("tm")
    me = p * NC + c

    barrier = pltpu.get_barrier_semaphore()

    def signal(dz, dc, dp):
        pl.semaphore_signal(barrier, inc=1, device_id=(dz, dc, dp), device_id_type=MESH)

    @pl.loop(1, 2 * NC)
    def _(d):
        other = lax.rem(me + d, 2 * NC)
        signal(z, lax.rem(other, NC), other // NC)

    @pl.loop(1, NZ)
    def _(d):
        signal(lax.rem(z + d, NZ), c, p)

    zr = lax.rem(z + 1, NZ)
    zl = lax.rem(z + NZ - 1, NZ)
    signal(zr, c, 1 - p)
    signal(zl, c, 1 - p)

    tabs = [
        pltpu.make_async_copy(f_hbm, f_ref, tab_sem.at[0]),
        pltpu.make_async_copy(ih_hbm, ih_ref, tab_sem.at[1]),
        pltpu.make_async_copy(il_hbm, il_ref, tab_sem.at[2]),
    ]
    for t in tabs:
        t.start()

    mask = mask_ref[...].astype(F32)
    diag = jnp.where(iota((ROWS, ROWS), 0) == iota((ROWS, ROWS), 1), mask, 0.0).astype(BF)
    clean = mm(diag, raw_ref[...]).astype(BF)
    clean_ref[...] = clean
    rows = iota((128, 256), 0)
    pick = (rows % 4) * 64 + p * 32 + rows // 4 == iota((128, 256), 1)
    tg_ref[z] = mm(jnp.where(pick, 1.0, 0.0).astype(BF), tmpl_ref[...].reshape(256, TL)).astype(BF)

    pl.semaphore_wait(barrier, 2 * NC - 1 + NZ - 1 + 2)

    up = lax.rem(c + NC - 1, NC)
    down = lax.rem(c + 1, NC)
    halos = [
        pltpu.make_async_remote_copy(
            src_ref=clean_ref.at[pl.ds(0, 16)], dst_ref=halo_ref.at[1],
            send_sem=halo_send.at[0], recv_sem=halo_recv.at[0],
            device_id=(z, up, p), device_id_type=MESH),
        pltpu.make_async_remote_copy(
            src_ref=clean_ref.at[pl.ds(48, 16)], dst_ref=halo_ref.at[0],
            send_sem=halo_send.at[1], recv_sem=halo_recv.at[1],
            device_id=(z, down, p), device_id_type=MESH),
    ]
    for h in halos:
        h.start()

    def right(s):
        slot = lax.rem(z - s + NZ, NZ)
        return pltpu.make_async_remote_copy(
            src_ref=tg_ref.at[slot], dst_ref=tg_ref.at[slot],
            send_sem=ring_send.at[0, s], recv_sem=ring_recv.at[0, s],
            device_id=(zr, c, p), device_id_type=MESH)

    def left(s):
        slot = lax.rem(z + s, NZ)
        return pltpu.make_async_remote_copy(
            src_ref=tg_ref.at[slot], dst_ref=tg_ref.at[slot],
            send_sem=ring_send.at[1, s], recv_sem=ring_recv.at[1, s],
            device_id=(zl, c, p), device_id_type=MESH)

    def forward(s):
        right(s - 1).wait_recv()
        right(s).start()
        left(s - 1).wait_recv()
        if s < 3:
            left(s).start()

    right(0).start()
    left(0).start()

    lane128 = iota((64, 128), 1)
    row64 = iota((64, 128), 0)
    bias = column(benc_ref, 16, 128)
    hi = bias.astype(BF).astype(F32)
    mid = (bias - hi).astype(BF).astype(F32)
    low = bias - hi - mid
    four = lambda x: jnp.concatenate([x] * 4, axis=0)
    fixed = jnp.where(lane128 == 6, four(hi), 0.0)
    fixed = jnp.where(lane128 == 14, four(mid), fixed)
    fixed = jnp.where(lane128 == 22, four(low), fixed)
    fixed = jnp.where((lane128 == 7) & (row64 < 16), BIG, fixed)
    fixed = jnp.where((lane128 == 15) & (row64 >= 48), BIG, fixed)
    base1 = jnp.concatenate([mm(wenc_ref[...], q1_ref[v]) for v in range(4)], axis=0)
    for r in range(8):
        w1_ref[pl.ds(r * 64, 64), :] = (
            (pltpu.roll(base1, 8 * r, 1) if r else base1) + fixed
        ).astype(BF)
    base2 = mm(wmid_ref[...], q2_ref[...])
    for r in range(8):
        w2_ref[pl.ds(r * 32, 32), :] = (
            pltpu.roll(base2, 48 * r, 1) if r else base2
        ).astype(BF)
    w3s_ref[...] = jnp.zeros(w3s_ref.shape, BF)
    for n in range(4):
        base3 = mm(wdec_ref[...], q3_ref[n])
        skip = base3[:, :256].astype(BF)
        wide = jnp.concatenate([base3[:, 256:], jnp.zeros((16, 256), F32)], axis=1)
        for r in range(4):
            w3s_ref[pl.ds(r * 64 + n * 16, 16), pl.ds(128 * r, 256)] = skip
            w3m_ref[pl.ds(r * 64 + n * 16, 16), :] = (
                pltpu.roll(wide, 96 * r, 1) if r else wide
            ).astype(BF)
    b2_ref[...] = column(bmid_ref, 32, HALF)
    b3_ref[...] = column(bdec_ref, 16, HALF)
    rep = (iota((16, 256), 1) % 16 == iota((16, 256), 0)).astype(F32).astype(BF)
    wrow = mm(wout_ref[...], rep)
    orow = iota((16, 256), 0)
    block = (orow % 8 // 2) * 4 + orow // 8 * 2 + orow % 2
    wo = jnp.where(iota((16, 256), 1) // 16 == block, wrow, 0.0).astype(BF)
    scol = iota((TL, TL), 1)
    split = jnp.where(
        iota((TL, TL), 0) == (scol % HALF) * 2 + scol // HALF, 1.0, 0.0
    ).astype(BF)
    own_ref[...] = mm(clean, split)
    alive_ref[...] = mm(diag, jnp.ones((ROWS, HALF), BF))

    for h in halos:
        h.wait_recv()
    prow = iota((80, 16), 0)
    pcol = iota((80, 16), 1)
    above = jnp.where((prow + 11 == pcol) & (c > 0), 1.0, 0.0).astype(BF)
    below = jnp.where((prow == pcol + 69) & (pcol < 5) & (c < NC - 1), 1.0, 0.0).astype(BF)
    inner = jnp.where(iota((80, 64), 0) == iota((80, 64), 1) + 5, 1.0, 0.0).astype(BF)
    tall = mm(inner, clean) + mm(above, halo_ref[0]) + mm(below, halo_ref[1])
    parted = mm(tall.astype(BF), split)
    even = parted[:, :HALF]
    odd = parted[:, HALF:]
    lane80 = iota((80, HALF), 1)
    later = lambda x, lanes: jnp.where(lanes == 0, 0.0, pltpu.roll(x, 1, 1))
    sooner = lambda x, lanes: jnp.where(lanes == HALF - 1, 0.0, pltpu.roll(x, HALF - 1, 1))
    slots = [later(even, lane80), later(odd, lane80), even, odd, sooner(even, lane80), sooner(odd, lane80)]
    slots.append(jnp.ones((80, HALF), F32))
    edge = jnp.where(iota((80, HALF), 0) % 2 == 0, 0, HALF - 1)
    slots.append(jnp.where(lane80 == edge, 1.0, 0.0))
    for n in range(8):
        for h in range(2):
            cv_ref[h, pl.ds(n, 80, stride=8), :] = slots[n][:, h * 128 : (h + 1) * 128]

    @pl.loop(0, 9)
    def _(q):
        first = pl.multiple_of(q * 64, 64)
        for h in range(2):
            window = cv_ref[h, pl.ds(first, 128), :].astype(BF)
            e = mm(w1_ref[...], window)
            ev_ref[pl.ds(pl.multiple_of(q * 512, 512), 512), h * 128 : (h + 1) * 128] = (
                jnp.maximum(e, 0.0).astype(BF)
            )

    @pl.when(c == 0)
    def _():
        ev_ref[0:256, :] = jnp.zeros((256, HALF), BF)

    @pl.when(c == NC - 1)
    def _():
        ev_ref[68 * 64 : 72 * 64, :] = jnp.zeros((256, HALF), BF)

    forward(1)

    lane16 = iota((16, HALF), 1)

    @pl.loop(0, 36, unroll=4)
    def _(i):
        first = pl.multiple_of(i * 128, 128)
        part = lambda o: ev_ref[pl.ds(first + o, 16), :].astype(F32)
        pooled = (part(16) + part(32) + part(80) + part(96)) * 0.25
        at = pl.multiple_of(i * 48, 16)
        pv_ref[pl.ds(at, 16), :] = later(pooled, lane16).astype(BF)
        pv_ref[pl.ds(at + 16, 16), :] = pooled.astype(BF)
        pv_ref[pl.ds(at + 32, 16), :] = sooner(pooled, lane16).astype(BF)

    lane32 = iota((32, HALF), 1)

    def middle(first_row, count, acc):
        for r in range(count):
            m = jnp.maximum(acc[r * 32 : (r + 1) * 32] + b2_ref[...], 0.0)
            at = pl.multiple_of((first_row + r) * 96, 32)
            mv_ref[pl.ds(at, 32), :] = later(m, lane32).astype(BF)
            mv_ref[pl.ds(at + 32, 32), :] = m.astype(BF)
            mv_ref[pl.ds(at + 64, 32), :] = sooner(m, lane32).astype(BF)

    @pl.loop(0, 4)
    def _(q):
        window = pv_ref[pl.ds(pl.multiple_of(q * 384, 128), 480), :]
        middle(q * 8, 8, mm(w2_ref[:, :480], window))

    middle(32, 2, mm(w2_ref[0:64, :192], pv_ref[pl.ds(1536, 192), :]))

    @pl.when(c == 0)
    def _():
        mv_ref[0:96, :] = jnp.zeros((96, HALF), BF)

    @pl.when(c == NC - 1)
    def _():
        mv_ref[33 * 96 : 34 * 96, :] = jnp.zeros((96, HALF), BF)

    forward(2)

    @pl.loop(0, 8)
    def _(q):
        skips = ev_ref[pl.ds(pl.multiple_of(q * 512, 512) + 192, 640), :]
        mids = mv_ref[pl.ds(pl.multiple_of(q * 384, 128), 576), :]
        acc = mm(w3s_ref[...], skips) + mm(w3m_ref[:, :576], mids)
        acc = acc.reshape(16, 16, HALF) + b3_ref[...][None]
        decoded = jnp.maximum(acc, 0.0).astype(BF).reshape(256, HALF)
        branch = mm(wo, decoded)
        here = pl.ds(pl.multiple_of(q * 8, 8), 8)
        alive = alive_ref[here, :]
        for ps in range(2):
            lanes = slice(ps * HALF, (ps + 1) * HALF)
            dp_ref[here, lanes] = alive * (
                own_ref[here, lanes] + branch[ps * 8 : ps * 8 + 8] + bout_ref[0]
            )

    forward(3)

    natural = lax.dot_general(
        dp_ref[...].astype(BF), split, (((1,), (1,)), ((), ())), preferred_element_type=F32
    ).astype(BF)
    den_ref[...] = natural
    sd_ref[...] = natural.reshape(2, 32, TL)

    to_partner = pltpu.make_async_remote_copy(
        src_ref=sd_ref.at[1 - p], dst_ref=xw_ref.at[p],
        send_sem=x_send.at[0], recv_sem=x_recv.at[0],
        device_id=(z, c, 1 - p), device_id_type=MESH)
    to_partner.start()

    def to_previous(h):
        return pltpu.make_async_remote_copy(
            src_ref=sd_ref.at[h], dst_ref=xw_ref.at[2],
            send_sem=x_send.at[1 + h], recv_sem=x_recv.at[1],
            device_id=(zl, c, h), device_id_type=MESH)

    @pl.when(p == 0)
    def _():
        to_previous(0).start()
        to_previous(1).start()

    xw_ref[p] = sd_ref[p]

    tabs[0].wait()
    for s in range(1):
        right(3).wait_recv()

    @pl.loop(0, NZ)
    def _(k):
        ts_ref[k] = mm(tg_ref[k], f_ref[...])

    to_partner.wait_recv()
    to_previous(0).wait_recv()
    rrow = iota((128, 32), 0)
    repeat = jnp.where(rrow // 4 == iota((128, 32), 1), 1.0, 0.0).astype(BF)
    lane1k = iota((128, 2 * TL), 1)
    sign = jnp.where((lane1k % 2 == 1), -1.0, 1.0)
    spectra = []
    for n in range(3):
        block_rows = xw_ref[n]
        if n == 2:
            block_rows = block_rows * jnp.where(z == NZ - 1, 0.0, 1.0).astype(BF)
        spectra.append(mm(mm(repeat, block_rows).astype(BF), f_ref[...]))
    z_ref[0] = spectra[0] + sign * spectra[1]
    z_ref[1] = spectra[1] + sign * spectra[2]

    lane512 = iota((8, TL), 1)

    @pl.loop(0, NZ)
    def _(k):
        for n in range(2):
            a = jnp.zeros((8, TL), F32)
            b = jnp.zeros((8, TL), F32)
            d = jnp.zeros((8, TL), F32)
            for s in range(16):
                here = pl.ds(s * 8, 8)
                tr = ts_ref[k, here, 0:TL]
                ti = ts_ref[k, here, TL : 2 * TL]
                sr = z_ref[n, here, 0:TL]
                si = z_ref[n, here, TL : 2 * TL]
                a = a + sr * tr
                b = b + si * ti
                d = d + (si * tr - sr * ti)
            a = a + pltpu.roll(a, 4, 0)
            b = b + pltpu.roll(b, 4, 0)
            d = d + pltpu.roll(d, 4, 0)
            at = pl.ds(pl.multiple_of(n * 64 + k * 8, 8), 8)
            g_ref[at, 0:TL] = jnp.where(lane512 == 0, a, a + b)
            g_ref[at, TL : 2 * TL] = jnp.where(lane512 == 0, b, d)

    tabs[1].wait()
    tabs[2].wait()
    g = g_ref[...]
    g_hi = g.astype(BF)
    g_lo = (g - g_hi.astype(F32)).astype(BF)
    lags = mm(g_hi, ih_ref[...]) + (mm(g_lo, ih_ref[...]) + mm(g_hi, il_ref[...]))
    for t in range(4):
        lag_ref[t] = lags[:, t * 128 : (t + 1) * 128]

    lane8 = iota((8, 128), 1) // 32
    for n in range(2):
        for t in range(4):
            quarter = [lag_ref[t, pl.ds(n * 64 + k, 8, stride=8), :] for k in range(4)]
            for o in range(4):
                piece = jnp.zeros((8, 128), F32)
                for k in range(4):
                    shift = (k - o) % 4 * 32
                    moved = pltpu.roll(quarter[k], shift, 1) if shift else quarter[k]
                    piece = jnp.where(lane8 == k, moved, piece)
                rs_ref[n * NC + t * 4 + o] = piece

    def scatter(d):
        other = lax.rem(me + d, 2 * NC)
        return pltpu.make_async_remote_copy(
            src_ref=rs_ref.at[other], dst_ref=rr_ref.at[me],
            send_sem=rs_send.at[d], recv_sem=rs_recv.at[me],
            device_id=(z, lax.rem(other, NC), other // NC), device_id_type=MESH)

    def arrival(d):
        other = lax.rem(me + d, 2 * NC)
        return pltpu.make_async_remote_copy(
            src_ref=rs_ref.at[other], dst_ref=rr_ref.at[other],
            send_sem=rs_send.at[d], recv_sem=rs_recv.at[other],
            device_id=(z, lax.rem(other, NC), other // NC), device_id_type=MESH)

    @pl.loop(1, 2 * NC)
    def _(d):
        scatter(d).start()

    @pl.loop(1, 2 * NC)
    def _(d):
        arrival(d).wait_recv()

    total = lax.fori_loop(
        1, 2 * NC, lambda d, t: t + rr_ref[lax.rem(me + d, 2 * NC)], rs_ref[me]
    )
    as_ref[...] = total.reshape(8, 1, 128)

    def spread(d):
        other = lax.rem(z + d, NZ)
        return pltpu.make_async_remote_copy(
            src_ref=as_ref.at[other], dst_ref=ar_ref.at[z],
            send_sem=a_send.at[d], recv_sem=a_recv.at[z],
            device_id=(other, c, p), device_id_type=MESH)

    def landing(d):
        other = lax.rem(z + d, NZ)
        return pltpu.make_async_remote_copy(
            src_ref=as_ref.at[other], dst_ref=ar_ref.at[other],
            send_sem=a_send.at[d], recv_sem=a_recv.at[other],
            device_id=(other, c, p), device_id_type=MESH)

    @pl.loop(1, NZ)
    def _(d):
        spread(d).start()

    ar_ref[z] = as_ref[z]

    @pl.loop(1, NZ)
    def _(d):
        landing(d).wait_recv()

    found = ar_ref[...].reshape(8, 128)
    turned = [found] + [pltpu.roll(found, 128 - 32 * k, 1) for k in range(1, 4)]
    for r in range(4):
        local = lax.rem(assign_ref[r], 4)
        row = jnp.zeros((8, 128), F32)
        for k in range(4):
            row = row + jnp.where(local == k, 1.0, 0.0) * turned[k]
        corr_ref[r] = row[:, :32]

    for h in halos:
        h.wait_send()
    for s in range(4):
        right(s).wait_send()
        if s < 3:
            left(s).wait_send()
    to_partner.wait_send()

    @pl.when(p == 0)
    def _():
        to_previous(0).wait_send()
        to_previous(1).wait_send()

    @pl.loop(1, 2 * NC)
    def _(d):
        scatter(d).wait_send()

    @pl.loop(1, NZ)
    def _(d):
        spread(d).wait_send()


def body(raw, dead_mask, templates, assign, w_enc, b_enc, w_mid, b_mid, w_dec, b_dec, w_out, b_out):
    hi, lo = lag_table()
    vm = pl.BlockSpec(memory_space=pltpu.VMEM)
    sm = pl.BlockSpec(memory_space=pltpu.SMEM)
    hbm = pl.BlockSpec(memory_space=pl.ANY)
    dma = pltpu.SemaphoreType.DMA
    denoised, corr = pl.pallas_call(
        kernel,
        out_shape=(
            jax.ShapeDtypeStruct((ROWS, TL), BF),
            jax.ShapeDtypeStruct((4, 8, 32), F32),
        ),
        in_specs=[vm, vm, vm, sm, vm, sm, vm, sm, vm, sm, vm, sm, vm, vm, vm, hbm, hbm, hbm],
        out_specs=(vm, vm),
        scratch_shapes=[
            pltpu.VMEM((TL, 2 * TL), BF),
            pltpu.VMEM((2 * TL, TL), BF),
            pltpu.VMEM((2 * TL, TL), BF),
            pltpu.VMEM((ROWS, TL), BF),
            pltpu.VMEM((2, 16, TL), BF),
            pltpu.VMEM((2, 640, 128), F32),
            pltpu.VMEM((512, 128), BF),
            pltpu.VMEM((256, 512), BF),
            pltpu.VMEM((256, 640), BF),
            pltpu.VMEM((256, 640), BF),
            pltpu.VMEM((72 * 64, HALF), BF),
            pltpu.VMEM((36 * 48, HALF), BF),
            pltpu.VMEM((34 * 96, HALF), BF),
            pltpu.VMEM((ROWS, TL), F32),
            pltpu.VMEM((ROWS, TL), F32),
            pltpu.VMEM((ROWS, HALF), F32),
            pltpu.VMEM((32, HALF), F32),
            pltpu.VMEM((16, HALF), F32),
            pltpu.VMEM((NZ, 128, TL), BF),
            pltpu.VMEM((NZ, 128, 2 * TL), F32),
            pltpu.VMEM((2, 32, TL), BF),
            pltpu.VMEM((3, 32, TL), BF),
            pltpu.VMEM((2, 128, 2 * TL), F32),
            pltpu.VMEM((128, 2 * TL), F32),
            pltpu.VMEM((4, 128, 128), F32),
            pltpu.VMEM((2 * NC, 8, 128), F32),
            pltpu.VMEM((2 * NC, 8, 128), F32),
            pltpu.VMEM((NZ, 1, 128), F32),
            pltpu.VMEM((NZ, 1, 128), F32),
            dma((3,)),
            dma((2,)),
            dma((2,)),
            dma((2, 4)),
            dma((2, 4)),
            dma((3,)),
            dma((2,)),
            dma((2 * NC,)),
            dma((2 * NC,)),
            dma((NZ,)),
            dma((NZ,)),
        ],
        compiler_params=pltpu.CompilerParams(
            collective_id=0, has_side_effects=True, vmem_limit_bytes=48 * 1024 * 1024
        ),
    )(
        raw,
        dead_mask.reshape(1, ROWS),
        templates,
        assign,
        w_enc.reshape(16, 9),
        b_enc,
        w_mid.reshape(32, 144),
        b_mid,
        w_dec.reshape(16, 432),
        b_dec,
        w_out.reshape(1, 16),
        b_out,
        jnp.asarray(encoder_table(), BF),
        jnp.asarray(middle_table(), BF),
        jnp.asarray(decoder_table(), BF),
        jnp.asarray(spectrum_table(), BF),
        jnp.asarray(hi),
        jnp.asarray(lo),
    )
    return denoised, corr.reshape(4, 8, 1, 32)


def solution(mesh):
    return jax.shard_map(
        body,
        mesh=mesh,
        in_specs=(
            P("chan", ("tmpl", "tm")),
            P("chan"),
            P("tmpl", "chan", None),
            P("tmpl"),
            P(),
            P(),
            P(),
            P(),
            P(),
            P(),
            P(),
            P(),
        ),
        out_specs=(P("chan", ("tmpl", "tm")), P("tmpl", None, "tm", "chan")),
        check_vma=False,
    )
```

time: 437 us -> 67.5 us (0.15)
  the two profiles are of different devices: /device:TPU:4 before, /device:TPU:1 now
where the time goes in v1:
time: 67.5 us; the launch traced here: 66.9 us
  Pallas kernels  48.9 us (72%)
  local copies, waits for them, and re-layouts  16.6 us (25%)
  between operations  1.33 us (2%)
    pallas_call x1, Pallas kernels, body(): pl.pallas_call(kernel, out_shape=(jax.ShapeDtypeStruct((ROWS, TL), BF), j...  48.9 us
    unnamed x32, local copies, waits for them, and re-layouts  15.6 us

profile of v1, /device:TPU:1, one launch (start us, length us, event | category | flops | bytes accessed | tf_op | source)
XLA Modules:
  0.0 66.9 jit_solution(1605813063184905590)
XLA Ops:
  0.6 0.9 %copy.25 = bf16[16,48,3,3]{0,3,2,1:T(4,128)(2,1)S(1)} copy(bf16[16,48,3,3]{1,0,3,2:T(8,128)(2,1)} %param.26) | data formatting | bytes 27648 | tf_op args[8]
  1.5 0.1 reshape.25
  1.6 0.1 copy.28.wdec_ref
  1.7 0.8 %copy.24 = bf16[32,16,3,3]{0,3,2,1:T(4,128)(2,1)S(1)} copy(bf16[32,16,3,3]{0,1,3,2:T(8,128)(2,1)} %param.24) | data formatting | bytes 18432 | tf_op args[6]
  2.5 0.1 copy.27.wmid_ref
  2.6 0.7 %reshape.23 = bf16[16,9]{0,1:T(8,128)(2,1)S(1)} reshape(bf16[16,1,3,3]{0,3,2,1:T(4,128)(2,1)} %param.22) | data formatting | bytes 576 | tf_op jit(solution)/shard_map/reshape | solution.py:575
  3.3 0.1 copy.26.wenc_ref
  4.1 0.0 copy-start
  4.1 1.6 %copy-done = bf16[4,432,640]{2,1,0:T(8,128)(2,1)S(1)} copy-done((bf16[4,432,640]{2,1,0:T(8,128)(2,1)S(1)}, bf16[4,432,640]{2,1,0:T(8,128)(2,1)}, u32[]{:S(2)}) %copy-start) | copy-done | bytes 2211864
  5.7 0.0 copy-start.1
  5.7 1.2 %copy-done.1 = bf16[512,1024]{1,0:T(8,128)(2,1)S(1)} copy-done((bf16[512,1024]{1,0:T(8,128)(2,1)S(1)}, bf16[512,1024]{1,0:T(8,128)(2,1)}, u32[]{:S(2)}) %copy-start.1) | copy-done | bytes 1048600
  6.9 0.0 copy-start.2
  6.9 1.2 %copy-done.2 = bf16[1024,512]{1,0:T(8,128)(2,1)S(1)} copy-done((bf16[1024,512]{1,0:T(8,128)(2,1)S(1)}, bf16[1024,512]{1,0:T(8,128)(2,1)}, u32[]{:S(2)}) %copy-start.2) | copy-done | bytes 1048600
  8.2 0.0 copy-start.3
  8.2 1.2 %copy-done.3 = bf16[1024,512]{1,0:T(8,128)(2,1)S(1)} copy-done((bf16[1024,512]{1,0:T(8,128)(2,1)S(1)}, bf16[1024,512]{1,0:T(8,128)(2,1)}, u32[]{:S(2)}) %copy-start.3) | copy-done | bytes 1048600
  9.4 0.0 copy-start.4
  9.4 0.9 %copy-done.4 = bf16[4,64,512]{2,1,0:T(8,128)(2,1)S(1)} copy-done((bf16[4,64,512]{2,1,0:T(8,128)(2,1)S(1)}, bf16[4,64,512]{2,1,0:T(8,128)(2,1)}, u32[]{:S(2)}) %copy-start.4) | copy-done | bytes 262168
  10.3 0.0 copy-start.5
  10.3 0.9 %copy-done.5 = bf16[144,512]{1,0:T(8,128)(2,1)S(1)} copy-done((bf16[144,512]{1,0:T(8,128)(2,1)S(1)}, bf16[144,512]{1,0:T(8,128)(2,1)}, u32[]{:S(2)}) %copy-start.5) | copy-done | bytes 147480
  11.2 0.0 copy-start.6
  11.2 0.8 %copy-done.6 = bf16[64,512]{1,0:T(8,128)(2,1)S(1)} copy-done((bf16[64,512]{1,0:T(8,128)(2,1)S(1)}, bf16[64,512]{1,0:T(8,128)(2,1)}, u32[]{:S(2)}) %copy-start.6) | copy-done | bytes 65560
  12.1 0.0 copy-start.7
  12.1 0.7 %copy-done.7 = bf16[4,9,128]{2,1,0:T(8,128)(2,1)S(1)} copy-done((bf16[4,9,128]{2,1,0:T(8,128)(2,1)S(1)}, bf16[4,9,128]{2,1,0:T(8,128)(2,1)}, u32[]{:S(2)}) %copy-start.7) | copy-done | bytes 9240
  12.8 0.0 copy-start.8
  12.8 0.7 copy-done.8
  13.5 0.0 copy-start.9
  13.5 0.7 copy-done.9
  14.1 0.0 copy-start.10
  14.1 0.7 copy-done.10
  14.8 0.0 copy-start.11
  14.8 0.7 copy-done.11
  15.4 0.0 copy-start.12
  15.4 0.7 copy-done.12
  16.1 0.0 copy-start.13
  16.1 0.7 copy-done.13
  16.7 48.9 %shard_map.185 = (bf16[64,512]{1,0:T(8,128)(2,1)S(1)}, f32[4,8,32]{2,1,0:T(8,128)S(1)}) custom-call(bf16[64,512]{1,0:T(8,128)(2,1)S(1)} %copy-done.6, s32[1,64]{1,0:T(1,128)S(1)} %bitcast.12, bf16[4,64,512]{2,1,0:T(8,128)(2,1)S(1)} %copy-done.4, s32[4]{0:T(128)S(1)} %copy-done.9, bf16[16,9]{1,0:T(8,128)(2,1)S(1)} %copy.26.wenc_ref, f32[16]{0:T(128)S(1)} %copy-done.10, ...), custom_call_target="tpu_custom_call" | custom-call | tf_op jit(solution)/shard_map/pallas_call | solution.py:517
  65.7 0.6 copy.33
  66.3 0.6 copy.34
  (1 shorter events, 0.0 us)
Async XLA Ops:
  4.1 1.6 %copy-start = (bf16[4,432,640]{2,1,0:T(8,128)(2,1)S(1)}, bf16[4,432,640]{2,1,0:T(8,128)(2,1)}, u32[]{:S(2)}) copy-start(bf16[4,432,640]{2,1,0:T(8,128)(2,1)} %constant.14.clone.q3_ref) | copy-start | bytes 6635524
  5.7 1.2 %copy-start.1 = (bf16[512,1024]{1,0:T(8,128)(2,1)S(1)}, bf16[512,1024]{1,0:T(8,128)(2,1)}, u32[]{:S(2)}) copy-start(bf16[512,1024]{1,0:T(8,128)(2,1)} %constant.15.clone.f_hbm) | copy-start | bytes 3145732
  6.9 1.2 %copy-start.2 = (bf16[1024,512]{1,0:T(8,128)(2,1)S(1)}, bf16[1024,512]{1,0:T(8,128)(2,1)}, u32[]{:S(2)}) copy-start(bf16[1024,512]{1,0:T(8,128)(2,1)} %constant.16.clone.ih_hbm) | copy-start | bytes 3145732
  8.2 1.2 %copy-start.3 = (bf16[1024,512]{1,0:T(8,128)(2,1)S(1)}, bf16[1024,512]{1,0:T(8,128)(2,1)}, u32[]{:S(2)}) copy-start(bf16[1024,512]{1,0:T(8,128)(2,1)} %constant.17.clone.il_hbm) | copy-start | bytes 3145732
  9.4 0.9 %copy-start.4 = (bf16[4,64,512]{2,1,0:T(8,128)(2,1)S(1)}, bf16[4,64,512]{2,1,0:T(8,128)(2,1)}, u32[]{:S(2)}) copy-start(bf16[4,64,512]{2,1,0:T(8,128)(2,1)} %tmpl_ref.1) | copy-start | bytes 786436
  10.3 0.9 %copy-start.5 = (bf16[144,512]{1,0:T(8,128)(2,1)S(1)}, bf16[144,512]{1,0:T(8,128)(2,1)}, u32[]{:S(2)}) copy-start(bf16[144,512]{1,0:T(8,128)(2,1)} %constant.13.clone.q2_ref) | copy-start | bytes 442372
  11.2 0.8 %copy-start.6 = (bf16[64,512]{1,0:T(8,128)(2,1)S(1)}, bf16[64,512]{1,0:T(8,128)(2,1)}, u32[]{:S(2)}) copy-start(bf16[64,512]{1,0:T(8,128)(2,1)} %raw_ref.1) | copy-start | bytes 196612
  12.1 0.7 %copy-start.7 = (bf16[4,9,128]{2,1,0:T(8,128)(2,1)S(1)}, bf16[4,9,128]{2,1,0:T(8,128)(2,1)}, u32[]{:S(2)}) copy-start(bf16[4,9,128]{2,1,0:T(8,128)(2,1)} %constant.12.clone.q1_ref) | copy-start | bytes 27652
  12.8 0.7 copy-start.8
  13.5 0.7 copy-start.9
  14.1 0.7 copy-start.10
  14.8 0.7 copy-start.11
  15.4 0.7 copy-start.12
  16.1 0.7 copy-start.13

commit v2 on v1

v2 whole, which is shorter than its diff:
```python
import functools
import math

import jax
import jax.numpy as jnp
import numpy as np
from jax import lax
from jax.experimental import pallas as pl
from jax.experimental.pallas import tpu as pltpu
from jax.sharding import PartitionSpec as P

BF = jnp.bfloat16
F32 = jnp.float32
MESH = pl.DeviceIdType.MESH
ROWS = 64
TL = 512
HALF = 256
NZ = 8
NC = 16
BIG = -1e30


def middle_table():
    q = np.zeros((3, 3, 16, 512), np.float32)
    for g in range(16):
        for rr in range(3):
            for v in range(3):
                q[rr, v, g, rr * 48 + v * 16 + g] = 1
    return q.reshape(144, 512)


def encoder_table():
    q = np.zeros((4, 3, 3, 128), np.float32)
    for v in range(4):
        for rr in range(3):
            for dt in range(3):
                q[v, rr, dt, rr * 8 + v + dt] = 1
    return q.reshape(4, 9, 128)


def decoder_tables():
    qs = np.zeros((4, 3, 3, 16, 256), np.float32)
    qm = np.zeros((4, 3, 3, 32, 384), np.float32)
    for ps in range(2):
        for pr in range(2):
            n = ps * 2 + pr
            for rr in range(4):
                for v in range(4):
                    if 0 <= rr - pr <= 2 and 0 <= v - ps <= 2:
                        for g in range(16):
                            qs[n, rr - pr, v - ps, g, rr * 64 + v * 16 + g] = 1
            for dr in range(3):
                for dt in range(3):
                    rr = (pr + dr - 1) // 2 + 1
                    v = (ps + dt - 1) // 2 + 1
                    for m in range(32):
                        qm[n, dr, dt, m, rr * 96 + v * 32 + m] = 1
    return qs.reshape(4, 144, 256), qm.reshape(4, 288, 384)


def spectrum_table():
    s = np.arange(TL)[:, None]
    f = np.arange(TL)[None, :]
    phase = ((s * f) % (2 * TL)) * (math.pi / TL)
    re = np.cos(phase)
    im = -np.sin(phase)
    im[:, 0] = np.where(np.arange(TL) % 2 == 0, 1.0, -1.0)
    return np.concatenate([re, im], axis=1).astype(np.float32)


def lag_table():
    f = np.arange(TL)[:, None]
    j = np.arange(TL)[None, :]
    phase = ((f * j) % (2 * TL)) * (math.pi / TL)
    re = np.cos(phase) * 2
    im = -np.sin(phase) * 2
    re[0] = 1
    im[0] = np.where(np.arange(TL) % 2 == 0, 1.0, -1.0)
    return (np.concatenate([re, im], axis=0) / (2 * TL)).astype(np.float32)


def iota(shape, dim):
    return lax.broadcasted_iota(jnp.int32, shape, dim)


def mm(a, b):
    return jnp.dot(a, b, preferred_element_type=F32)


def column(ref, count, lanes):
    rows = iota((count, lanes), 0)
    out = jnp.zeros((count, lanes), F32)
    for g in range(count):
        out = jnp.where(rows == g, ref[g], out)
    return out


def kernel(
    raw_hbm, mask_hbm, tmpl_hbm, assign_hbm, wenc_hbm, benc_hbm, wmid_hbm, bmid_hbm,
    wdec_hbm, bdec_hbm, wout_hbm, bout_hbm, q1_hbm, q2_hbm, q3s_hbm, q3m_hbm, f_hbm, i_hbm,
    den_ref, corr_ref,
    raw_ref, mask_ref, tmpl_ref, assign_ref, wenc_ref, benc_ref, wmid_ref, bmid_ref,
    wdec_ref, bdec_ref, wout_ref, bout_ref, q1_ref, q2_ref, q3s_ref, q3m_ref, f_ref, i_ref,
    clean_ref, halo_ref, cv_ref, w1_ref, w2_ref, w3s_ref, w3m_ref,
    ev_ref, pv_ref, mv_ref, dp_ref, own_ref, alive_ref, b2_ref, b3_ref, tg_ref, ts_ref, sd_ref, xw_ref,
    xr_ref, z_ref, g_ref, lag_ref, rs_ref, rr_ref, as_ref, ar_ref,
    tab_sem, halo_send, halo_recv, ring_send, ring_recv, x_send, x_recv,
    rs_send, rs_recv, a_send, a_recv,
):
    z = lax.axis_index("tmpl")
    c = lax.axis_index("chan")
    p = lax.axis_index("tm")
    me = p * NC + c
    zr = lax.rem(z + 1, NZ)
    zl = lax.rem(z + NZ - 1, NZ)

    loads = {}
    for n, (name, source, target) in enumerate([
        ("raw", raw_hbm, raw_ref), ("mask", mask_hbm, mask_ref), ("tmpl", tmpl_hbm, tmpl_ref),
        ("wenc", wenc_hbm, wenc_ref), ("q1", q1_hbm, q1_ref), ("benc", benc_hbm, benc_ref),
        ("wmid", wmid_hbm, wmid_ref), ("q2", q2_hbm, q2_ref), ("bmid", bmid_hbm, bmid_ref),
        ("wdec", wdec_hbm, wdec_ref), ("q3s", q3s_hbm, q3s_ref), ("q3m", q3m_hbm, q3m_ref),
        ("bdec", bdec_hbm, bdec_ref), ("wout", wout_hbm, wout_ref), ("bout", bout_hbm, bout_ref),
        ("f", f_hbm, f_ref), ("assign", assign_hbm, assign_ref), ("i", i_hbm, i_ref),
    ]):
        loads[name] = pltpu.make_async_copy(source, target, tab_sem.at[n])
        loads[name].start()

    def ready(*names):
        for name in names:
            loads[name].wait()

    barrier = pltpu.get_barrier_semaphore()

    def signal(dz, dc, dp):
        pl.semaphore_signal(barrier, inc=1, device_id=(dz, dc, dp), device_id_type=MESH)

    @pl.loop(1, 2 * NC)
    def _(d):
        other = lax.rem(me + d, 2 * NC)
        signal(z, lax.rem(other, NC), other // NC)

    @pl.loop(1, NZ)
    def _(d):
        signal(lax.rem(z + d, NZ), c, p)

    signal(zr, c, 1 - p)
    signal(zl, c, 1 - p)

    ready("raw", "mask")
    mask = mask_ref[...].astype(F32)
    diag = jnp.where(iota((ROWS, ROWS), 0) == iota((ROWS, ROWS), 1), mask, 0.0).astype(BF)
    clean = mm(diag, raw_ref[...]).astype(BF)
    clean_ref[...] = clean

    pl.semaphore_wait(barrier, 2 * NC - 1 + NZ - 1 + 2)

    up = lax.rem(c + NC - 1, NC)
    down = lax.rem(c + 1, NC)
    halos = [
        pltpu.make_async_remote_copy(
            src_ref=clean_ref.at[pl.ds(0, 16)], dst_ref=halo_ref.at[1],
            send_sem=halo_send.at[0], recv_sem=halo_recv.at[0],
            device_id=(z, up, p), device_id_type=MESH),
        pltpu.make_async_remote_copy(
            src_ref=clean_ref.at[pl.ds(48, 16)], dst_ref=halo_ref.at[0],
            send_sem=halo_send.at[1], recv_sem=halo_recv.at[1],
            device_id=(z, down, p), device_id_type=MESH),
    ]
    for h in halos:
        h.start()

    ready("tmpl")
    rows = iota((128, 256), 0)
    pick = (rows % 4) * 64 + p * 32 + rows // 4 == iota((128, 256), 1)
    tg_ref[0] = mm(jnp.where(pick, 1.0, 0.0).astype(BF), tmpl_ref[...].reshape(256, TL)).astype(BF)

    def right(s):
        part = pl.ds(0, 64 if s == 3 else 128)
        return pltpu.make_async_remote_copy(
            src_ref=tg_ref.at[s, part], dst_ref=tg_ref.at[s + 1, part],
            send_sem=ring_send.at[0, s], recv_sem=ring_recv.at[0, s],
            device_id=(zr, c, p), device_id_type=MESH)

    def left(s):
        part = pl.ds(64, 64) if s == 3 else pl.ds(0, 128)
        return pltpu.make_async_remote_copy(
            src_ref=tg_ref.at[(NZ - s) % NZ, part], dst_ref=tg_ref.at[NZ - 1 - s, part],
            send_sem=ring_send.at[1, s], recv_sem=ring_recv.at[1, s],
            device_id=(zl, c, p), device_id_type=MESH)

    def forward(s):
        right(s - 1).wait_recv()
        right(s).start()
        left(s - 1).wait_recv()
        left(s).start()

    right(0).start()
    left(0).start()

    scol = iota((TL, TL), 1)
    split = jnp.where(
        iota((TL, TL), 0) == (scol % HALF) * 2 + scol // HALF, 1.0, 0.0
    ).astype(BF)
    later = lambda x, lanes: jnp.where(lanes == 0, 0.0, pltpu.roll(x, 1, 1))
    sooner = lambda x, lanes: jnp.where(lanes == HALF - 1, 0.0, pltpu.roll(x, HALF - 1, 1))

    def variants(tall):
        parted = mm(tall.astype(BF), split)
        even = parted[:, :HALF]
        odd = parted[:, HALF:]
        lanes = iota(even.shape, 1)
        return [
            later(even, lanes), later(odd, lanes), even, odd, sooner(even, lanes), sooner(odd, lanes)
        ]

    inner = jnp.where(iota((80, 64), 0) == iota((80, 64), 1) + 5, 1.0, 0.0).astype(BF)
    slots = variants(mm(inner, clean))
    slots.append(jnp.ones((80, HALF), F32))
    edge = jnp.where(iota((80, HALF), 0) % 2 == 0, 0, HALF - 1)
    slots.append(jnp.where(iota((80, HALF), 1) == edge, 1.0, 0.0))
    for n in range(8):
        for h in range(2):
            cv_ref[h, pl.ds(n, 80, stride=8), :] = slots[n][:, h * 128 : (h + 1) * 128]

    ready("wenc", "q1", "benc")
    lane128 = iota((64, 128), 1)
    row64 = iota((64, 128), 0)
    bias = column(benc_ref, 16, 128)
    hi = bias.astype(BF).astype(F32)
    mid = (bias - hi).astype(BF).astype(F32)
    low = bias - hi - mid
    four = lambda x: jnp.concatenate([x] * 4, axis=0)
    fixed = jnp.where(lane128 == 6, four(hi), 0.0)
    fixed = jnp.where(lane128 == 14, four(mid), fixed)
    fixed = jnp.where(lane128 == 22, four(low), fixed)
    fixed = jnp.where((lane128 == 7) & (row64 < 16), BIG, fixed)
    fixed = jnp.where((lane128 == 15) & (row64 >= 48), BIG, fixed)
    wenc = jnp.concatenate([wenc_ref[r] for r in range(3)], axis=0)
    over = lambda w, q: lax.dot_general(w, q, (((0,), (0,)), ((), ())), preferred_element_type=F32)
    base1 = jnp.concatenate([over(wenc, q1_ref[v]) for v in range(4)], axis=0)
    for r in range(8):
        w1_ref[pl.ds(r * 64, 64), :] = (
            (pltpu.roll(base1, 8 * r, 1) if r else base1) + fixed
        ).astype(BF)

    def encode(q):
        first = pl.multiple_of(q * 64, 64)
        for h in range(2):
            window = cv_ref[h, pl.ds(first, 128), :].astype(BF)
            e = mm(w1_ref[...], window)
            ev_ref[pl.ds(pl.multiple_of(q * 512, 512), 512), h * 128 : (h + 1) * 128] = (
                jnp.maximum(e, 0.0).astype(BF)
            )

    pl.loop(1, 8)(encode)

    lane16 = iota((16, HALF), 1)

    def pool(i):
        first = pl.multiple_of(i * 128, 128)
        part = lambda o: ev_ref[pl.ds(first + o, 16), :].astype(F32)
        pooled = (part(16) + part(32) + part(80) + part(96)) * 0.25
        at = pl.multiple_of(i * 48, 16)
        pv_ref[pl.ds(at, 16), :] = later(pooled, lane16).astype(BF)
        pv_ref[pl.ds(at + 16, 16), :] = pooled.astype(BF)
        pv_ref[pl.ds(at + 32, 16), :] = sooner(pooled, lane16).astype(BF)

    pl.loop(4, 32, unroll=4)(pool)

    for h in halos:
        h.wait_recv()
    far = iota((24, 16), 0)
    far = jnp.where(far < 8, far, far + 56)
    away = iota((24, 16), 1)
    above = jnp.where((far + 11 == away) & (c > 0), 1.0, 0.0).astype(BF)
    below = jnp.where((far == away + 69) & (away < 5) & (c < NC - 1), 1.0, 0.0).astype(BF)
    near = iota((24, 64), 0)
    near = jnp.where(near < 8, near, near + 56)
    kept = jnp.where(near == iota((24, 64), 1) + 5, 1.0, 0.0).astype(BF)
    edges = variants(mm(kept, clean) + mm(above, halo_ref[0]) + mm(below, halo_ref[1]))
    for n in range(6):
        for h in range(2):
            cut = edges[n][:, h * 128 : (h + 1) * 128]
            cv_ref[h, pl.ds(n, 8, stride=8), :] = cut[:8]
            cv_ref[h, pl.ds(512 + n, 16, stride=8), :] = cut[8:]
    encode(0)
    encode(8)

    @pl.when(c == 0)
    def _():
        ev_ref[0:256, :] = jnp.zeros((256, HALF), BF)

    @pl.when(c == NC - 1)
    def _():
        ev_ref[68 * 64 : 72 * 64, :] = jnp.zeros((256, HALF), BF)

    for i in (0, 1, 2, 3, 32, 33, 34, 35):
        pool(i)

    forward(1)

    ready("wmid", "q2", "bmid")
    base2 = over(wmid_ref[...].reshape(144, 32), q2_ref[...])
    for r in range(8):
        w2_ref[pl.ds(r * 32, 32), :] = (
            pltpu.roll(base2, 48 * r, 1) if r else base2
        ).astype(BF)
    b2_ref[...] = column(bmid_ref, 32, HALF)

    lane32 = iota((32, HALF), 1)

    def middle(first_row, count, acc):
        for r in range(count):
            m = jnp.maximum(acc[r * 32 : (r + 1) * 32] + b2_ref[...], 0.0)
            at = pl.multiple_of((first_row + r) * 96, 32)
            mv_ref[pl.ds(at, 32), :] = later(m, lane32).astype(BF)
            mv_ref[pl.ds(at + 32, 32), :] = m.astype(BF)
            mv_ref[pl.ds(at + 64, 32), :] = sooner(m, lane32).astype(BF)

    @pl.loop(0, 4)
    def _(q):
        window = pv_ref[pl.ds(pl.multiple_of(q * 384, 128), 480), :]
        middle(q * 8, 8, mm(w2_ref[:, :480], window))

    middle(32, 2, mm(w2_ref[0:64, :192], pv_ref[pl.ds(1536, 192), :]))

    @pl.when(c == 0)
    def _():
        mv_ref[0:96, :] = jnp.zeros((96, HALF), BF)

    @pl.when(c == NC - 1)
    def _():
        mv_ref[33 * 96 : 34 * 96, :] = jnp.zeros((96, HALF), BF)

    ready("wdec", "q3s", "q3m", "bdec", "wout", "bout")
    taps = [wdec_ref[dr, dt] for dr in range(3) for dt in range(3)]
    wskip = jnp.concatenate([t[:, 32:] for t in taps], axis=1)
    wup = jnp.concatenate([t[:, :32] for t in taps], axis=1)
    w3s_ref[...] = jnp.zeros(w3s_ref.shape, BF)
    for n in range(4):
        skip = mm(wskip, q3s_ref[n]).astype(BF)
        wide = jnp.concatenate([mm(wup, q3m_ref[n]), jnp.zeros((16, 256), F32)], axis=1)
        for r in range(4):
            w3s_ref[pl.ds(r * 64 + n * 16, 16), pl.ds(128 * r, 256)] = skip
            w3m_ref[pl.ds(r * 64 + n * 16, 16), :] = (
                pltpu.roll(wide, 96 * r, 1) if r else wide
            ).astype(BF)
    b3_ref[...] = column(bdec_ref, 16, HALF)
    rep = (iota((16, 256), 1) % 16 == iota((16, 256), 0)).astype(F32).astype(BF)
    wrow = mm(wout_ref[...], rep)
    orow = iota((16, 256), 0)
    block = (orow % 8 // 2) * 4 + orow // 8 * 2 + orow % 2
    wo = jnp.where(iota((16, 256), 1) // 16 == block, wrow, 0.0).astype(BF)
    own_ref[...] = mm(clean, split)
    alive_ref[...] = mm(diag, jnp.ones((ROWS, HALF), BF))

    def decode(q):
        skips = ev_ref[pl.ds(pl.multiple_of(q * 512, 512) + 192, 640), :]
        mids = mv_ref[pl.ds(pl.multiple_of(q * 384, 128), 576), :]
        acc = mm(w3s_ref[...], skips) + mm(w3m_ref[:, :576], mids)
        acc = acc.reshape(16, 16, HALF) + b3_ref[...][None]
        decoded = jnp.maximum(acc, 0.0).astype(BF).reshape(256, HALF)
        branch = mm(wo, decoded)
        here = pl.ds(pl.multiple_of(q * 8, 8), 8)
        alive = alive_ref[here, :]
        for ps in range(2):
            lanes = slice(ps * HALF, (ps + 1) * HALF)
            dp_ref[here, lanes] = alive * (
                own_ref[here, lanes] + branch[ps * 8 : ps * 8 + 8] + bout_ref[0]
            )

    def finish(h):
        here = pl.ds(pl.multiple_of(h * 32, 32), 32)
        natural = lax.dot_general(
            dp_ref[here, :].astype(BF), split, (((1,), (1,)), ((), ())), preferred_element_type=F32
        ).astype(BF)
        den_ref[here, :] = natural
        sd_ref[h] = natural

    to_partner = pltpu.make_async_remote_copy(
        src_ref=sd_ref.at[1 - p], dst_ref=xw_ref.at[p],
        send_sem=x_send.at[0], recv_sem=x_recv.at[0],
        device_id=(z, c, 1 - p), device_id_type=MESH)

    def to_previous(h):
        return pltpu.make_async_remote_copy(
            src_ref=sd_ref.at[h], dst_ref=xw_ref.at[2],
            send_sem=x_send.at[1 + h], recv_sem=x_recv.at[1],
            device_id=(zl, c, h), device_id_type=MESH)

    other_half = (1 - p) * 4
    pl.loop(other_half, other_half + 4)(decode)
    finish(1 - p)
    to_partner.start()

    @pl.when(p == 0)
    def _():
        to_previous(1).start()

    forward(2)

    own_half = p * 4
    pl.loop(own_half, own_half + 4)(decode)
    finish(p)

    @pl.when(p == 0)
    def _():
        to_previous(0).start()

    xw_ref[p] = sd_ref[p]

    forward(3)

    ready("f")
    wide3 = mm(tg_ref[0:4].reshape(512, TL), f_ref[...])
    ts_ref[0:4] = wide3.reshape(4, 128, 2 * TL)
    wide3 = mm(tg_ref[5:8].reshape(384, TL), f_ref[...])
    ts_ref[5:8] = wide3.reshape(3, 128, 2 * TL)
    right(3).wait_recv()
    left(3).wait_recv()
    ts_ref[4] = mm(tg_ref[4], f_ref[...])

    rrow = iota((128, 32), 0)
    repeat = jnp.where(rrow // 4 == iota((128, 32), 1), 1.0, 0.0).astype(BF)
    lane1k = iota((128, 2 * TL), 1)
    sign = jnp.where((lane1k % 2 == 1), -1.0, 1.0)
    to_partner.wait_recv()
    to_previous(0).wait_recv()
    for n in range(3):
        block_rows = xw_ref[n]
        if n == 2:
            block_rows = block_rows * jnp.where(z == NZ - 1, 0.0, 1.0).astype(BF)
        xr_ref[pl.ds(n * 128, 128), :] = mm(repeat, block_rows).astype(BF)
    spectra = mm(xr_ref[...], f_ref[...])
    z_ref[0] = spectra[0:128] + sign * spectra[128:256]
    z_ref[1] = spectra[128:256] + sign * spectra[256:384]

    lane512 = iota((8, TL), 1)

    @pl.loop(0, NZ)
    def _(k):
        for n in range(2):
            a = jnp.zeros((8, TL), F32)
            b = jnp.zeros((8, TL), F32)
            d = jnp.zeros((8, TL), F32)
            for s in range(16):
                here = pl.ds(s * 8, 8)
                tr = ts_ref[k, here, 0:TL]
                ti = ts_ref[k, here, TL : 2 * TL]
                sr = z_ref[n, here, 0:TL]
                si = z_ref[n, here, TL : 2 * TL]
                a = a + sr * tr
                b = b + si * ti
                d = d + (si * tr - sr * ti)
            a = a + pltpu.roll(a, 4, 0)
            b = b + pltpu.roll(b, 4, 0)
            d = d + pltpu.roll(d, 4, 0)
            at = pl.ds(pl.multiple_of(n * 64 + k * 8, 8), 8)
            g_ref[at, 0:TL] = jnp.where(lane512 == 0, a, a + b)
            g_ref[at, TL : 2 * TL] = jnp.where(lane512 == 0, b, d)

    ready("i")
    lags = mm(g_ref[...].astype(BF), i_ref[...])
    for t in range(4):
        lag_ref[t] = lags[:, t * 128 : (t + 1) * 128]

    lane8 = iota((8, 128), 1) // 32
    for n in range(2):
        for t in range(4):
            quarter = [lag_ref[t, pl.ds(n * 64 + k, 8, stride=8), :] for k in range(4)]
            for o in range(4):
                piece = jnp.zeros((8, 128), F32)
                for k in range(4):
                    shift = (k - o) % 4 * 32
                    moved = pltpu.roll(quarter[k], shift, 1) if shift else quarter[k]
                    piece = jnp.where(lane8 == k, moved, piece)
                rs_ref[n * NC + t * 4 + o] = piece

    @pl.loop(1, 2 * NC)
    def _(d):
        other = lax.rem(me + d, 2 * NC)
        pltpu.make_async_remote_copy(
            src_ref=rs_ref.at[other], dst_ref=rr_ref.at[d - 1],
            send_sem=rs_send.at[0], recv_sem=rs_recv.at[0],
            device_id=(z, lax.rem(other, NC), other // NC), device_id_type=MESH).start()

    shares = pltpu.make_async_remote_copy(
        src_ref=rr_ref, dst_ref=rr_ref, send_sem=rs_send.at[0], recv_sem=rs_recv.at[0],
        device_id=(z, c, 1 - p), device_id_type=MESH)
    shares.wait_recv()
    parts = [rs_ref[me]] + [rr_ref[d] for d in range(2 * NC - 1)]
    while len(parts) > 1:
        parts = [parts[n] + parts[n + 1] for n in range(0, len(parts), 2)]
    as_ref[...] = parts[0].reshape(8, 1, 128)

    for d in range(1, NZ):
        pltpu.make_async_remote_copy(
            src_ref=as_ref.at[d], dst_ref=ar_ref.at[z],
            send_sem=a_send.at[d], recv_sem=a_recv.at[z],
            device_id=(lax.rem(z + NZ - d, NZ), c, p), device_id_type=MESH).start()

    ar_ref[z] = as_ref[0]

    def landing(d):
        other = lax.rem(z + d, NZ)
        return pltpu.make_async_remote_copy(
            src_ref=as_ref.at[d], dst_ref=ar_ref.at[other],
            send_sem=a_send.at[d], recv_sem=a_recv.at[other],
            device_id=(other, c, p), device_id_type=MESH)

    for d in range(1, NZ):
        landing(d).wait_recv()

    found = ar_ref[...].reshape(8, 128)
    turned = [found] + [pltpu.roll(found, 128 - 32 * k, 1) for k in range(1, 4)]
    ready("assign")
    for r in range(4):
        local = lax.rem(assign_ref[r], 4)
        row = jnp.zeros((8, 128), F32)
        for k in range(4):
            row = row + jnp.where(local == k, 1.0, 0.0) * turned[k]
        corr_ref[r] = row[:, :32].reshape(8, 1, 32)

    for h in halos:
        h.wait_send()
    for s in range(4):
        right(s).wait_send()
        left(s).wait_send()
    to_partner.wait_send()

    @pl.when(p == 0)
    def _():
        to_previous(0).wait_send()
        to_previous(1).wait_send()

    shares.wait_send()
    for d in range(1, NZ):
        landing(d).wait_send()


def body(raw, dead_mask, templates, assign, w_enc, b_enc, w_mid, b_mid, w_dec, b_dec, w_out, b_out):
    vm = pl.BlockSpec(memory_space=pltpu.VMEM)
    hbm = pl.BlockSpec(memory_space=pltpu.HBM)
    dma = pltpu.SemaphoreType.DMA
    q3s, q3m = decoder_tables()
    tables = [
        jnp.asarray(t, BF)
        for t in (encoder_table(), middle_table(), q3s, q3m, spectrum_table(), lag_table())
    ]
    operands = [
        raw,
        dead_mask.reshape(1, ROWS),
        templates,
        assign,
        w_enc.transpose(1, 2, 3, 0).reshape(3, 3, 16),
        b_enc,
        w_mid.transpose(2, 3, 1, 0),
        b_mid,
        w_dec.transpose(2, 3, 0, 1),
        b_dec,
        w_out.reshape(1, 16),
        b_out,
    ] + tables
    scalars = (3, 5, 7, 9, 11)
    landing_places = [
        (pltpu.SMEM if n in scalars else pltpu.VMEM)(x.shape, x.dtype)
        for n, x in enumerate(operands)
    ]
    return pl.pallas_call(
        kernel,
        out_shape=(
            jax.ShapeDtypeStruct((ROWS, TL), BF),
            jax.ShapeDtypeStruct((4, 8, 1, 32), F32),
        ),
        in_specs=[hbm] * len(operands),
        out_specs=(vm, vm),
        scratch_shapes=landing_places + [
            pltpu.VMEM((ROWS, TL), BF),
            pltpu.VMEM((2, 16, TL), BF),
            pltpu.VMEM((2, 640, 128), F32),
            pltpu.VMEM((512, 128), BF),
            pltpu.VMEM((256, 512), BF),
            pltpu.VMEM((256, 640), BF),
            pltpu.VMEM((256, 640), BF),
            pltpu.VMEM((72 * 64, HALF), BF),
            pltpu.VMEM((36 * 48, HALF), BF),
            pltpu.VMEM((34 * 96, HALF), BF),
            pltpu.VMEM((ROWS, TL), F32),
            pltpu.VMEM((ROWS, TL), F32),
            pltpu.VMEM((ROWS, HALF), F32),
            pltpu.VMEM((32, HALF), F32),
            pltpu.VMEM((16, HALF), F32),
            pltpu.VMEM((NZ, 128, TL), BF),
            pltpu.VMEM((NZ, 128, 2 * TL), F32),
            pltpu.VMEM((2, 32, TL), BF),
            pltpu.VMEM((3, 32, TL), BF),
            pltpu.VMEM((384, TL), BF),
            pltpu.VMEM((2, 128, 2 * TL), F32),
            pltpu.VMEM((128, 2 * TL), F32),
            pltpu.VMEM((4, 128, 128), F32),
            pltpu.VMEM((2 * NC, 8, 128), F32),
            pltpu.VMEM((2 * NC - 1, 8, 128), F32),
            pltpu.VMEM((NZ, 1, 128), F32),
            pltpu.VMEM((NZ, 1, 128), F32),
            dma((len(operands),)),
            dma((2,)),
            dma((2,)),
            dma((2, 4)),
            dma((2, 4)),
            dma((3,)),
            dma((2,)),
            dma((1,)),
            dma((1,)),
            dma((NZ,)),
            dma((NZ,)),
        ],
        compiler_params=pltpu.CompilerParams(
            collective_id=0, has_side_effects=True, vmem_limit_bytes=56 * 1024 * 1024
        ),
    )(*operands)


def solution(mesh):
    return jax.shard_map(
        body,
        mesh=mesh,
        in_specs=(
            P("chan", ("tmpl", "tm")),
            P("chan"),
            P("tmpl", "chan", None),
            P("tmpl"),
            P(),
            P(),
            P(),
            P(),
            P(),
            P(),
            P(),
            P(),
        ),
        out_specs=(P("chan", ("tmpl", "tm")), P("tmpl", None, "tm", "chan")),
        check_vma=False,
    )
```

time: 67.5 us -> 47.9 us (0.71)
  local copies, waits for them, and re-layouts: 16.6 us -> 2.09 us
  Pallas kernels: 48.9 us -> 44.4 us
    unnamed x32 -> x4, local copies, waits for them, and re-layouts: 15.6 us -> 2.09 us
    pallas_call x1, Pallas kernels: 48.9 us -> 44.4 us  [body(): pl.pallas_call(kernel, out_shape=(jax.ShapeDtypeStruct((ROWS, TL), BF), j...]
    reshape x6 -> x0, local copies, waits for them, and re-layouts: 1.08 us -> none  [the longest x2 0.82 us: body(): w_enc.reshape(16, 9)]
where the time goes in v2:
time: 47.9 us; the launch traced here: 47.8 us
  Pallas kernels  44.4 us (93%)
  local copies, waits for them, and re-layouts  2.09 us (4%)
  between operations  1.3 us (3%)
    pallas_call x1, Pallas kernels, body(): pl.pallas_call(kernel, out_shape=(jax.ShapeDtypeStruct((ROWS, TL), BF), j...  44.4 us
    unnamed x4, local copies, waits for them, and re-layouts  2.09 us

profile of v2, /device:TPU:1, one launch (start us, length us, event | category | flops | bytes accessed | tf_op | source)
XLA Modules:
  0.0 47.8 jit_solution(7296668748590387365)
XLA Ops:
  1.3 44.4 %shard_map.185 = (bf16[64,512]{1,0:T(8,128)(2,1)}, f32[4,8,1,32]{3,2,1,0:T(1,128)}) custom-call(bf16[64,512]{1,0:T(8,128)(2,1)} %raw_hbm.1, s32[1,64]{1,0:T(1,128)} %bitcast.10, bf16[4,64,512]{2,1,0:T(8,128)(2,1)} %tmpl_hbm.1, s32[4]{0:T(128)} %assign_hbm.1, bf16[3,3,16]{2,1,0:T(4,128)(2,1)} %bitcast.9, f32[16]{0:T(128)} %benc_hbm.1, ...), custom_call_target="tpu_custom_call" | custom-call | tf_op jit(solution)/shard_map/pallas_call | solution.py:570
  45.7 0.0 copy-start
  45.7 1.5 %copy.23 = bf16[64,512]{1,0:T(8,128)(2,1)} copy(bf16[64,512]{1,0:T(8,128)(2,1)} %get-tuple-element.4) | data formatting | bytes 131072
  47.2 0.0 copy-done
  47.2 0.6 %copy.24 = f32[4,8,1,32]{3,2,1,0:T(1,128)} copy(f32[4,8,1,32]{3,2,1,0:T(1,128)S(1)} %copy-done) | data formatting | bytes 8192
Async XLA Ops:
  45.7 1.5 %copy-start = (f32[4,8,1,32]{3,2,1,0:T(1,128)S(1)}, f32[4,8,1,32]{3,2,1,0:T(1,128)}, u32[]{:S(2)}) copy-start(f32[4,8,1,32]{3,2,1,0:T(1,128)} %get-tuple-element.5) | copy-start | bytes 12292

commit v3 on v2

--- a/solution.py
+++ b/solution.py
@@ -104,7 +104,7 @@
     clean_ref, halo_ref, cv_ref, w1_ref, w2_ref, w3s_ref, w3m_ref,
     ev_ref, pv_ref, mv_ref, dp_ref, own_ref, alive_ref, b2_ref, b3_ref, tg_ref, ts_ref, sd_ref, xw_ref,
     xr_ref, z_ref, g_ref, lag_ref, rs_ref, rr_ref, as_ref, ar_ref,
-    tab_sem, halo_send, halo_recv, ring_send, ring_recv, x_send, x_recv,
+    tab_sem, den_sem, halo_send, halo_recv, ring_send, ring_recv, x_send, x_recv,
     rs_send, rs_recv, a_send, a_recv,
 ):
     z = lax.axis_index("tmpl")
@@ -152,6 +152,11 @@
     diag = jnp.where(iota((ROWS, ROWS), 0) == iota((ROWS, ROWS), 1), mask, 0.0).astype(BF)
     clean = mm(diag, raw_ref[...]).astype(BF)
     clean_ref[...] = clean
+
+    ready("tmpl")
+    rows = iota((128, 256), 0)
+    pick = (rows % 4) * 64 + p * 32 + rows // 4 == iota((128, 256), 1)
+    tg_ref[0] = mm(jnp.where(pick, 1.0, 0.0).astype(BF), tmpl_ref[...].reshape(256, TL)).astype(BF)
 
     pl.semaphore_wait(barrier, 2 * NC - 1 + NZ - 1 + 2)
 
@@ -170,33 +175,29 @@
     for h in halos:
         h.start()
 
-    ready("tmpl")
-    rows = iota((128, 256), 0)
-    pick = (rows % 4) * 64 + p * 32 + rows // 4 == iota((128, 256), 1)
-    tg_ref[0] = mm(jnp.where(pick, 1.0, 0.0).astype(BF), tmpl_ref[...].reshape(256, TL)).astype(BF)
-
-    def right(s):
-        part = pl.ds(0, 64 if s == 3 else 128)
+    def right(s, n):
+        part = pl.ds(n * 64, 64)
         return pltpu.make_async_remote_copy(
-            src_ref=tg_ref.at[s, part], dst_ref=tg_ref.at[s + 1, part],
-            send_sem=ring_send.at[0, s], recv_sem=ring_recv.at[0, s],
+            src_ref=tg_ref.at[max(2 * s - 1, 0), part], dst_ref=tg_ref.at[2 * s + 1, part],
+            send_sem=ring_send.at[0, 2 * s + n], recv_sem=ring_recv.at[0, 2 * s + n],
             device_id=(zr, c, p), device_id_type=MESH)
 
-    def left(s):
-        part = pl.ds(64, 64) if s == 3 else pl.ds(0, 128)
+    def left(s, n):
+        part = pl.ds(n * 64, 64)
         return pltpu.make_async_remote_copy(
-            src_ref=tg_ref.at[(NZ - s) % NZ, part], dst_ref=tg_ref.at[NZ - 1 - s, part],
-            send_sem=ring_send.at[1, s], recv_sem=ring_recv.at[1, s],
+            src_ref=tg_ref.at[2 * s, part], dst_ref=tg_ref.at[min(2 * s + 2, 7), part],
+            send_sem=ring_send.at[1, 2 * s + n], recv_sem=ring_recv.at[1, 2 * s + n],
             device_id=(zl, c, p), device_id_type=MESH)
 
-    def forward(s):
-        right(s - 1).wait_recv()
-        right(s).start()
-        left(s - 1).wait_recv()
-        left(s).start()
-
-    right(0).start()
-    left(0).start()
+    def forward(s, n):
+        right(s - 1, n).wait_recv()
+        right(s, n).start()
+        left(s - 1, 1 - n).wait_recv()
+        left(s, 1 - n).start()
+
+    for n in range(2):
+        right(0, n).start()
+        left(0, 1 - n).start()
 
     scol = iota((TL, TL), 1)
     split = jnp.where(
@@ -268,38 +269,6 @@
 
     pl.loop(4, 32, unroll=4)(pool)
 
-    for h in halos:
-        h.wait_recv()
-    far = iota((24, 16), 0)
-    far = jnp.where(far < 8, far, far + 56)
-    away = iota((24, 16), 1)
-    above = jnp.where((far + 11 == away) & (c > 0), 1.0, 0.0).astype(BF)
-    below = jnp.where((far == away + 69) & (away < 5) & (c < NC - 1), 1.0, 0.0).astype(BF)
-    near = iota((24, 64), 0)
-    near = jnp.where(near < 8, near, near + 56)
-    kept = jnp.where(near == iota((24, 64), 1) + 5, 1.0, 0.0).astype(BF)
-    edges = variants(mm(kept, clean) + mm(above, halo_ref[0]) + mm(below, halo_ref[1]))
-    for n in range(6):
-        for h in range(2):
-            cut = edges[n][:, h * 128 : (h + 1) * 128]
-            cv_ref[h, pl.ds(n, 8, stride=8), :] = cut[:8]
-            cv_ref[h, pl.ds(512 + n, 16, stride=8), :] = cut[8:]
-    encode(0)
-    encode(8)
-
-    @pl.when(c == 0)
-    def _():
-        ev_ref[0:256, :] = jnp.zeros((256, HALF), BF)
-
-    @pl.when(c == NC - 1)
-    def _():
-        ev_ref[68 * 64 : 72 * 64, :] = jnp.zeros((256, HALF), BF)
-
-    for i in (0, 1, 2, 3, 32, 33, 34, 35):
-        pool(i)
-
-    forward(1)
-
     ready("wmid", "q2", "bmid")
     base2 = over(wmid_ref[...].reshape(144, 32), q2_ref[...])
     for r in range(8):
@@ -318,20 +287,11 @@
             mv_ref[pl.ds(at + 32, 32), :] = m.astype(BF)
             mv_ref[pl.ds(at + 64, 32), :] = sooner(m, lane32).astype(BF)
 
-    @pl.loop(0, 4)
-    def _(q):
+    def eight(q):
         window = pv_ref[pl.ds(pl.multiple_of(q * 384, 128), 480), :]
         middle(q * 8, 8, mm(w2_ref[:, :480], window))
 
-    middle(32, 2, mm(w2_ref[0:64, :192], pv_ref[pl.ds(1536, 192), :]))
-
-    @pl.when(c == 0)
-    def _():
-        mv_ref[0:96, :] = jnp.zeros((96, HALF), BF)
-
-    @pl.when(c == NC - 1)
-    def _():
-        mv_ref[33 * 96 : 34 * 96, :] = jnp.zeros((96, HALF), BF)
+    pl.loop(1, 3)(eight)
 
     ready("wdec", "q3s", "q3m", "bdec", "wout", "bout")
     taps = [wdec_ref[dr, dt] for dr in range(3) for dt in range(3)]
@@ -355,6 +315,8 @@
     own_ref[...] = mm(clean, split)
     alive_ref[...] = mm(diag, jnp.ones((ROWS, HALF), BF))
 
+    forward(1, 0)
+
     def decode(q):
         skips = ev_ref[pl.ds(pl.multiple_of(q * 512, 512) + 192, 640), :]
         mids = mv_ref[pl.ds(pl.multiple_of(q * 384, 128), 576), :]
@@ -370,13 +332,17 @@
                 own_ref[here, lanes] + branch[ps * 8 : ps * 8 + 8] + bout_ref[0]
             )
 
+    def results(h):
+        here = pl.ds(pl.multiple_of(h * 32, 32), 32)
+        return pltpu.make_async_copy(sd_ref.at[h], den_ref.at[here], den_sem.at[h])
+
     def finish(h):
         here = pl.ds(pl.multiple_of(h * 32, 32), 32)
         natural = lax.dot_general(
             dp_ref[here, :].astype(BF), split, (((1,), (1,)), ((), ())), preferred_element_type=F32
         ).astype(BF)
-        den_ref[here, :] = natural
         sd_ref[h] = natural
+        results(h).start()
 
     to_partner = pltpu.make_async_remote_copy(
         src_ref=sd_ref.at[1 - p], dst_ref=xw_ref.at[p],
@@ -389,8 +355,55 @@
             send_sem=x_send.at[1 + h], recv_sem=x_recv.at[1],
             device_id=(zl, c, h), device_id_type=MESH)
 
-    other_half = (1 - p) * 4
-    pl.loop(other_half, other_half + 4)(decode)
+    for q in (2, 3):
+        decode(q)
+    forward(1, 1)
+    decode(4)
+
+    for h in halos:
+        h.wait_recv()
+    far = iota((24, 16), 0)
+    far = jnp.where(far < 8, far, far + 56)
+    away = iota((24, 16), 1)
+    above = jnp.where((far + 11 == away) & (c > 0), 1.0, 0.0).astype(BF)
+    below = jnp.where((far == away + 69) & (away < 5) & (c < NC - 1), 1.0, 0.0).astype(BF)
+    near = iota((24, 64), 0)
+    near = jnp.where(near < 8, near, near + 56)
+    kept = jnp.where(near == iota((24, 64), 1) + 5, 1.0, 0.0).astype(BF)
+    edges = variants(mm(kept, clean) + mm(above, halo_ref[0]) + mm(below, halo_ref[1]))
+    for n in range(6):
+        for h in range(2):
+            cut = edges[n][:, h * 128 : (h + 1) * 128]
+            cv_ref[h, pl.ds(n, 8, stride=8), :] = cut[:8]
+            cv_ref[h, pl.ds(512 + n, 16, stride=8), :] = cut[8:]
+    encode(0)
+    encode(8)
+
+    @pl.when(c == 0)
+    def _():
+        ev_ref[0:256, :] = jnp.zeros((256, HALF), BF)
+
+    @pl.when(c == NC - 1)
+    def _():
+        ev_ref[68 * 64 : 72 * 64, :] = jnp.zeros((256, HALF), BF)
+
+    for i in (0, 1, 2, 3, 32, 33, 34, 35):
+        pool(i)
+
+    pl.loop(0, 4, step=3)(eight)
+    middle(32, 2, mm(w2_ref[0:64, :192], pv_ref[pl.ds(1536, 192), :]))
+
+    @pl.when(c == 0)
+    def _():
+        mv_ref[0:96, :] = jnp.zeros((96, HALF), BF)
+
+    @pl.when(c == NC - 1)
+    def _():
+        mv_ref[33 * 96 : 34 * 96, :] = jnp.zeros((96, HALF), BF)
+
+    pl.loop(5 * (1 - p), 5 * (1 - p) + 1)(decode)
+    forward(2, 0)
+    pl.loop(5 * (1 - p) + 1, 8 - 6 * p)(decode)
     finish(1 - p)
     to_partner.start()
 
@@ -398,10 +411,8 @@
     def _():
         to_previous(1).start()
 
-    forward(2)
-
-    own_half = p * 4
-    pl.loop(own_half, own_half + 4)(decode)
+    forward(2, 1)
+    pl.loop(5 * p, 2 + 6 * p)(decode)
     finish(p)
 
     @pl.when(p == 0)
@@ -410,55 +421,63 @@
 
     xw_ref[p] = sd_ref[p]
 
-    forward(3)
-
     ready("f")
-    wide3 = mm(tg_ref[0:4].reshape(512, TL), f_ref[...])
-    ts_ref[0:4] = wide3.reshape(4, 128, 2 * TL)
-    wide3 = mm(tg_ref[5:8].reshape(384, TL), f_ref[...])
-    ts_ref[5:8] = wide3.reshape(3, 128, 2 * TL)
-    right(3).wait_recv()
-    left(3).wait_recv()
-    ts_ref[4] = mm(tg_ref[4], f_ref[...])
+
+    def transform(first, count):
+        wide = mm(tg_ref[first : first + count].reshape(count * 128, TL), f_ref[...])
+        ts_ref[first : first + count] = wide.reshape(count, 128, 2 * TL)
+
+    transform(0, 5)
 
     rrow = iota((128, 32), 0)
     repeat = jnp.where(rrow // 4 == iota((128, 32), 1), 1.0, 0.0).astype(BF)
     lane1k = iota((128, 2 * TL), 1)
     sign = jnp.where((lane1k % 2 == 1), -1.0, 1.0)
     to_partner.wait_recv()
-    to_previous(0).wait_recv()
-    for n in range(3):
-        block_rows = xw_ref[n]
-        if n == 2:
-            block_rows = block_rows * jnp.where(z == NZ - 1, 0.0, 1.0).astype(BF)
-        xr_ref[pl.ds(n * 128, 128), :] = mm(repeat, block_rows).astype(BF)
+    for n in range(2):
+        xr_ref[pl.ds(n * 128, 128), :] = mm(repeat, xw_ref[n]).astype(BF)
     spectra = mm(xr_ref[...], f_ref[...])
     z_ref[0] = spectra[0:128] + sign * spectra[128:256]
-    z_ref[1] = spectra[128:256] + sign * spectra[256:384]
+    z_ref[1] = spectra[128:256]
+
+    forward(3, 0)
 
     lane512 = iota((8, TL), 1)
 
-    @pl.loop(0, NZ)
-    def _(k):
-        for n in range(2):
-            a = jnp.zeros((8, TL), F32)
-            b = jnp.zeros((8, TL), F32)
-            d = jnp.zeros((8, TL), F32)
-            for s in range(16):
-                here = pl.ds(s * 8, 8)
-                tr = ts_ref[k, here, 0:TL]
-                ti = ts_ref[k, here, TL : 2 * TL]
-                sr = z_ref[n, here, 0:TL]
-                si = z_ref[n, here, TL : 2 * TL]
-                a = a + sr * tr
-                b = b + si * ti
-                d = d + (si * tr - sr * ti)
-            a = a + pltpu.roll(a, 4, 0)
-            b = b + pltpu.roll(b, 4, 0)
-            d = d + pltpu.roll(d, 4, 0)
-            at = pl.ds(pl.multiple_of(n * 64 + k * 8, 8), 8)
-            g_ref[at, 0:TL] = jnp.where(lane512 == 0, a, a + b)
-            g_ref[at, TL : 2 * TL] = jnp.where(lane512 == 0, b, d)
+    def product(n, k):
+        a = jnp.zeros((8, TL), F32)
+        b = jnp.zeros((8, TL), F32)
+        d = jnp.zeros((8, TL), F32)
+        for s in range(16):
+            here = pl.ds(s * 8, 8)
+            tr = ts_ref[k, here, 0:TL]
+            ti = ts_ref[k, here, TL : 2 * TL]
+            sr = z_ref[n, here, 0:TL]
+            si = z_ref[n, here, TL : 2 * TL]
+            a = a + sr * tr
+            b = b + si * ti
+            d = d + (si * tr - sr * ti)
+        a = a + pltpu.roll(a, 4, 0)
+        b = b + pltpu.roll(b, 4, 0)
+        d = d + pltpu.roll(d, 4, 0)
+        at = pl.ds(pl.multiple_of(n * 64 + k * 8, 8), 8)
+        g_ref[at, 0:TL] = jnp.where(lane512 == 0, a, a + b)
+        g_ref[at, TL : 2 * TL] = jnp.where(lane512 == 0, b, d)
+
+    pl.loop(0, 5)(functools.partial(product, 0))
+    right(2, 1).wait_recv()
+    left(2, 0).wait_recv()
+    transform(5, 2)
+    pl.loop(5, 7)(functools.partial(product, 0))
+
+    to_previous(0).wait_recv()
+    following = xw_ref[2] * jnp.where(z == NZ - 1, 0.0, 1.0).astype(BF)
+    z_ref[1] = z_ref[1] + sign * mm(mm(repeat, following).astype(BF), f_ref[...])
+    pl.loop(0, 7)(functools.partial(product, 1))
+    right(3, 0).wait_recv()
+    left(3, 1).wait_recv()
+    transform(7, 1)
+    pl.loop(0, 2)(lambda n: product(n, 7))
 
     ready("i")
     lags = mm(g_ref[...].astype(BF), i_ref[...])
@@ -494,16 +513,17 @@
         parts = [parts[n] + parts[n + 1] for n in range(0, len(parts), 2)]
     as_ref[...] = parts[0].reshape(8, 1, 128)
 
+    places = [0, 1, -1, 2, -2, 3, -3, 4]
     for d in range(1, NZ):
         pltpu.make_async_remote_copy(
             src_ref=as_ref.at[d], dst_ref=ar_ref.at[z],
             send_sem=a_send.at[d], recv_sem=a_recv.at[z],
-            device_id=(lax.rem(z + NZ - d, NZ), c, p), device_id_type=MESH).start()
+            device_id=(lax.rem(z + NZ - places[d], NZ), c, p), device_id_type=MESH).start()
 
     ar_ref[z] = as_ref[0]
 
     def landing(d):
-        other = lax.rem(z + d, NZ)
+        other = lax.rem(z + NZ + places[d], NZ)
         return pltpu.make_async_remote_copy(
             src_ref=as_ref.at[d], dst_ref=ar_ref.at[other],
             send_sem=a_send.at[d], recv_sem=a_recv.at[other],
@@ -522,11 +542,16 @@
             row = row + jnp.where(local == k, 1.0, 0.0) * turned[k]
         corr_ref[r] = row[:, :32].reshape(8, 1, 32)
 
+    results(0).wait()
+    results(1).wait()
     for h in halos:
         h.wait_send()
-    for s in range(4):
-        right(s).wait_send()
-        left(s).wait_send()
+    for s in range(3):
+        for n in range(2):
+            right(s, n).wait_send()
+            left(s, n).wait_send()
+    right(3, 0).wait_send()
+    left(3, 1).wait_send()
     to_partner.wait_send()
 
     @pl.when(p == 0)
@@ -574,7 +599,7 @@
             jax.ShapeDtypeStruct((4, 8, 1, 32), F32),
         ),
         in_specs=[hbm] * len(operands),
-        out_specs=(vm, vm),
+        out_specs=(hbm, vm),
         scratch_shapes=landing_places + [
             pltpu.VMEM((ROWS, TL), BF),
             pltpu.VMEM((2, 16, TL), BF),
@@ -595,7 +620,7 @@
             pltpu.VMEM((NZ, 128, 2 * TL), F32),
             pltpu.VMEM((2, 32, TL), BF),
             pltpu.VMEM((3, 32, TL), BF),
-            pltpu.VMEM((384, TL), BF),
+            pltpu.VMEM((256, TL), BF),
             pltpu.VMEM((2, 128, 2 * TL), F32),
             pltpu.VMEM((128, 2 * TL), F32),
             pltpu.VMEM((4, 128, 128), F32),
@@ -606,8 +631,9 @@
             dma((len(operands),)),
             dma((2,)),
             dma((2,)),
-            dma((2, 4)),
-            dma((2, 4)),
+            dma((2,)),
+            dma((2, 8)),
+            dma((2, 8)),
             dma((3,)),
             dma((2,)),
             dma((1,)),

time: 47.9 us -> 43.7 us (0.912)
  Pallas kernels: 44.4 us -> 40.2 us
    pallas_call x1, Pallas kernels: 44.4 us -> 40.2 us  [body(): pl.pallas_call(kernel, out_shape=(jax.ShapeDtypeStruct((ROWS, TL), BF), j...]
where the time goes in v3:
time: 43.7 us; the launch traced here: 43.6 us
  Pallas kernels  40.2 us (92%)
  local copies, waits for them, and re-layouts  2.09 us (5%)
  between operations  1.3 us (3%)
    pallas_call x1, Pallas kernels, body(): pl.pallas_call(kernel, out_shape=(jax.ShapeDtypeStruct((ROWS, TL), BF), j...  40.2 us
    unnamed x4, local copies, waits for them, and re-layouts  2.09 us

profile of v3, /device:TPU:1, one launch (start us, length us, event | category | flops | bytes accessed | tf_op | source)
XLA Modules:
  0.0 43.6 jit_solution(3422043704165060767)
XLA Ops:
  1.3 40.2 %shard_map.185 = (bf16[64,512]{1,0:T(8,128)(2,1)}, f32[4,8,1,32]{3,2,1,0:T(1,128)}) custom-call(bf16[64,512]{1,0:T(8,128)(2,1)} %raw_hbm.1, s32[1,64]{1,0:T(1,128)} %bitcast.10, bf16[4,64,512]{2,1,0:T(8,128)(2,1)} %tmpl_hbm.1, s32[4]{0:T(128)} %assign_hbm.1, bf16[3,3,16]{2,1,0:T(4,128)(2,1)} %bitcast.9, f32[16]{0:T(128)} %benc_hbm.1, ...), custom_call_target="tpu_custom_call" | custom-call | tf_op jit(solution)/shard_map/pallas_call | solution.py:595
  41.5 0.0 copy-start
  41.5 1.5 %copy.23 = bf16[64,512]{1,0:T(8,128)(2,1)} copy(bf16[64,512]{1,0:T(8,128)(2,1)} %get-tuple-element.4) | data formatting | bytes 131072
  43.0 0.0 copy-done
  43.0 0.6 %copy.24 = f32[4,8,1,32]{3,2,1,0:T(1,128)} copy(f32[4,8,1,32]{3,2,1,0:T(1,128)S(1)} %copy-done) | data formatting | bytes 8192
Async XLA Ops:
  41.5 1.5 %copy-start = (f32[4,8,1,32]{3,2,1,0:T(1,128)S(1)}, f32[4,8,1,32]{3,2,1,0:T(1,128)}, u32[]{:S(2)}) copy-start(f32[4,8,1,32]{3,2,1,0:T(1,128)} %get-tuple-element.5) | copy-start | bytes 12292

commit v4 on v3

--- a/solution.py
+++ b/solution.py
@@ -38,9 +38,10 @@
     return q.reshape(4, 9, 128)
 
 
-def decoder_tables():
-    qs = np.zeros((4, 3, 3, 16, 256), np.float32)
-    qm = np.zeros((4, 3, 3, 32, 384), np.float32)
+def decoder_table():
+    q = np.zeros((4, 3, 3, 48, 640), np.float32)
+    skip_at = [96, 160, 320, 384]
+    up_at = [0, 224, 448]
     for ps in range(2):
         for pr in range(2):
             n = ps * 2 + pr
@@ -48,14 +49,14 @@
                 for v in range(4):
                     if 0 <= rr - pr <= 2 and 0 <= v - ps <= 2:
                         for g in range(16):
-                            qs[n, rr - pr, v - ps, g, rr * 64 + v * 16 + g] = 1
+                            q[n, rr - pr, v - ps, 32 + g, skip_at[rr] + v * 16 + g] = 1
             for dr in range(3):
                 for dt in range(3):
                     rr = (pr + dr - 1) // 2 + 1
                     v = (ps + dt - 1) // 2 + 1
                     for m in range(32):
-                        qm[n, dr, dt, m, rr * 96 + v * 32 + m] = 1
-    return qs.reshape(4, 144, 256), qm.reshape(4, 288, 384)
+                        q[n, dr, dt, m, up_at[rr] + v * 32 + m] = 1
+    return q.reshape(4, 432, 640)
 
 
 def spectrum_table():
@@ -97,15 +98,15 @@
 
 def kernel(
     raw_hbm, mask_hbm, tmpl_hbm, assign_hbm, wenc_hbm, benc_hbm, wmid_hbm, bmid_hbm,
-    wdec_hbm, bdec_hbm, wout_hbm, bout_hbm, q1_hbm, q2_hbm, q3s_hbm, q3m_hbm, f_hbm, i_hbm,
+    wdec_hbm, bdec_hbm, wout_hbm, bout_hbm, q1_hbm, q2_hbm, q3_hbm, f_hbm, i_hbm,
     den_ref, corr_ref,
     raw_ref, mask_ref, tmpl_ref, assign_ref, wenc_ref, benc_ref, wmid_ref, bmid_ref,
-    wdec_ref, bdec_ref, wout_ref, bout_ref, q1_ref, q2_ref, q3s_ref, q3m_ref, f_ref, i_ref,
-    clean_ref, halo_ref, cv_ref, w1_ref, w2_ref, w3s_ref, w3m_ref,
-    ev_ref, pv_ref, mv_ref, dp_ref, own_ref, alive_ref, b2_ref, b3_ref, tg_ref, ts_ref, sd_ref, xw_ref,
+    wdec_ref, bdec_ref, wout_ref, bout_ref, q1_ref, q2_ref, q3_ref, f_ref, i_ref,
+    clean_ref, halo_ref, cv_ref, w1_ref, w2_ref, wf_ref, w3_ref,
+    u_ref, pv_ref, dp_ref, own_ref, alive_ref, b2_ref, tg_ref, ts_ref, sd_ref, xw_ref,
     xr_ref, z_ref, g_ref, lag_ref, rs_ref, rr_ref, as_ref, ar_ref,
     tab_sem, den_sem, halo_send, halo_recv, ring_send, ring_recv, x_send, x_recv,
-    rs_send, rs_recv, a_send, a_recv,
+    rs_send, rs_recv, a_send, a_recv, hello_sem,
 ):
     z = lax.axis_index("tmpl")
     c = lax.axis_index("chan")
@@ -115,37 +116,46 @@
     zl = lax.rem(z + NZ - 1, NZ)
 
     loads = {}
-    for n, (name, source, target) in enumerate([
+    sources = [
         ("raw", raw_hbm, raw_ref), ("mask", mask_hbm, mask_ref), ("tmpl", tmpl_hbm, tmpl_ref),
         ("wenc", wenc_hbm, wenc_ref), ("q1", q1_hbm, q1_ref), ("benc", benc_hbm, benc_ref),
         ("wmid", wmid_hbm, wmid_ref), ("q2", q2_hbm, q2_ref), ("bmid", bmid_hbm, bmid_ref),
-        ("wdec", wdec_hbm, wdec_ref), ("q3s", q3s_hbm, q3s_ref), ("q3m", q3m_hbm, q3m_ref),
+        ("wdec", wdec_hbm, wdec_ref), ("q3", q3_hbm, q3_ref),
         ("bdec", bdec_hbm, bdec_ref), ("wout", wout_hbm, wout_ref), ("bout", bout_hbm, bout_ref),
         ("f", f_hbm, f_ref), ("assign", assign_hbm, assign_ref), ("i", i_hbm, i_ref),
-    ]):
-        loads[name] = pltpu.make_async_copy(source, target, tab_sem.at[n])
-        loads[name].start()
+    ]
+
+    def fetch(first, last):
+        for n in range(first, last):
+            name, source, target = sources[n]
+            loads[name] = pltpu.make_async_copy(source, target, tab_sem.at[n])
+            loads[name].start()
 
     def ready(*names):
         for name in names:
             loads[name].wait()
 
+    fetch(0, 3)
+
     barrier = pltpu.get_barrier_semaphore()
-
-    def signal(dz, dc, dp):
-        pl.semaphore_signal(barrier, inc=1, device_id=(dz, dc, dp), device_id_type=MESH)
-
-    @pl.loop(1, 2 * NC)
-    def _(d):
-        other = lax.rem(me + d, 2 * NC)
-        signal(z, lax.rem(other, NC), other // NC)
-
-    @pl.loop(1, NZ)
-    def _(d):
-        signal(lax.rem(z + d, NZ), c, p)
-
-    signal(zr, c, 1 - p)
-    signal(zl, c, 1 - p)
+    up = lax.rem(c + NC - 1, NC)
+    down = lax.rem(c + 1, NC)
+    flip = lambda n: c + n - 2 * n * lax.rem(c // n, 2)
+    partners = [(z, flip(n), p) for n in (1, 2, 4, 8)] + [(z, c, 1 - p)]
+    greeted = partners[1:] + [
+        (z, up, p), (z, down, p), (zr, c, p), (zl, c, p), (zr, c, 1 - p), (zl, c, 1 - p)
+    ]
+    for device in greeted:
+        pl.semaphore_signal(barrier, inc=1, device_id=device, device_id_type=MESH)
+    fetch(3, len(sources))
+
+    def greet(n):
+        pl.semaphore_signal(hello_sem.at[n], inc=1, device_id=partners[n], device_id_type=MESH)
+
+    def greeting(n):
+        pl.semaphore_wait(hello_sem.at[n], 1)
+        if n < 4:
+            greet(n + 1)
 
     ready("raw", "mask")
     mask = mask_ref[...].astype(F32)
@@ -158,10 +168,9 @@
     pick = (rows % 4) * 64 + p * 32 + rows // 4 == iota((128, 256), 1)
     tg_ref[0] = mm(jnp.where(pick, 1.0, 0.0).astype(BF), tmpl_ref[...].reshape(256, TL)).astype(BF)
 
-    pl.semaphore_wait(barrier, 2 * NC - 1 + NZ - 1 + 2)
-
-    up = lax.rem(c + NC - 1, NC)
-    down = lax.rem(c + 1, NC)
+    pl.semaphore_wait(barrier, len(greeted))
+    greet(0)
+
     halos = [
         pltpu.make_async_remote_copy(
             src_ref=clean_ref.at[pl.ds(0, 16)], dst_ref=halo_ref.at[1],
@@ -176,35 +185,40 @@
         h.start()
 
     def right(s, n):
-        part = pl.ds(n * 64, 64)
+        part = pl.ds(n * 32, 32)
         return pltpu.make_async_remote_copy(
             src_ref=tg_ref.at[max(2 * s - 1, 0), part], dst_ref=tg_ref.at[2 * s + 1, part],
-            send_sem=ring_send.at[0, 2 * s + n], recv_sem=ring_recv.at[0, 2 * s + n],
+            send_sem=ring_send.at[0, 4 * s + n], recv_sem=ring_recv.at[0, 4 * s + n],
             device_id=(zr, c, p), device_id_type=MESH)
 
     def left(s, n):
-        part = pl.ds(n * 64, 64)
+        part = pl.ds(96 - n * 32, 32)
         return pltpu.make_async_remote_copy(
             src_ref=tg_ref.at[2 * s, part], dst_ref=tg_ref.at[min(2 * s + 2, 7), part],
-            send_sem=ring_send.at[1, 2 * s + n], recv_sem=ring_recv.at[1, 2 * s + n],
+            send_sem=ring_send.at[1, 4 * s + n], recv_sem=ring_recv.at[1, 4 * s + n],
             device_id=(zl, c, p), device_id_type=MESH)
 
     def forward(s, n):
         right(s - 1, n).wait_recv()
         right(s, n).start()
-        left(s - 1, 1 - n).wait_recv()
-        left(s, 1 - n).start()
-
-    for n in range(2):
+        left(s - 1, n).wait_recv()
+        left(s, n).start()
+
+    def arrived(s, first, last):
+        for n in range(first, last):
+            right(s, n).wait_recv()
+            left(s, n).wait_recv()
+
+    for n in range(4):
         right(0, n).start()
-        left(0, 1 - n).start()
+        left(0, n).start()
 
     scol = iota((TL, TL), 1)
     split = jnp.where(
         iota((TL, TL), 0) == (scol % HALF) * 2 + scol // HALF, 1.0, 0.0
     ).astype(BF)
-    later = lambda x, lanes: jnp.where(lanes == 0, 0.0, pltpu.roll(x, 1, 1))
-    sooner = lambda x, lanes: jnp.where(lanes == HALF - 1, 0.0, pltpu.roll(x, HALF - 1, 1))
+    later = lambda x, lanes: jnp.where(lanes == 0, jnp.zeros_like(x), pltpu.roll(x, 1, 1))
+    sooner = lambda x, lanes: jnp.where(lanes == HALF - 1, jnp.zeros_like(x), pltpu.roll(x, HALF - 1, 1))
 
     def variants(tall):
         parted = mm(tall.astype(BF), split)
@@ -245,29 +259,40 @@
             (pltpu.roll(base1, 8 * r, 1) if r else base1) + fixed
         ).astype(BF)
 
+    def staggered(start, end, items):
+        held = None
+        for item in items:
+            value = start(item)
+            if held is not None:
+                end(*held)
+            held = (item, value)
+        end(*held)
+
     def encode(q):
-        first = pl.multiple_of(q * 64, 64)
-        for h in range(2):
-            window = cv_ref[h, pl.ds(first, 128), :].astype(BF)
-            e = mm(w1_ref[...], window)
-            ev_ref[pl.ds(pl.multiple_of(q * 512, 512), 512), h * 128 : (h + 1) * 128] = (
-                jnp.maximum(e, 0.0).astype(BF)
-            )
-
-    pl.loop(1, 8)(encode)
+        window = jnp.concatenate([cv_ref[h, q * 64 : q * 64 + 128, :] for h in range(2)], axis=1)
+        return mm(w1_ref[...], window.astype(BF))
+
+    def encoded(q, e):
+        e = jnp.maximum(e, 0.0).astype(BF)
+        for k in range(8):
+            at = (4 * q + k // 2) * 224 + k % 2 * 160
+            u_ref[at : at + 64, :] = e[k * 64 : (k + 1) * 64]
+
+    staggered(encode, encoded, range(1, 8))
 
     lane16 = iota((16, HALF), 1)
 
     def pool(i):
-        first = pl.multiple_of(i * 128, 128)
-        part = lambda o: ev_ref[pl.ds(first + o, 16), :].astype(F32)
-        pooled = (part(16) + part(32) + part(80) + part(96)) * 0.25
+        first = pl.multiple_of(i * 224, 16)
+        part = lambda o: u_ref[pl.ds(first + o, 16), :].astype(F32)
+        pooled = (part(16) + part(32) + part(176) + part(192)) * 0.25
         at = pl.multiple_of(i * 48, 16)
         pv_ref[pl.ds(at, 16), :] = later(pooled, lane16).astype(BF)
         pv_ref[pl.ds(at + 16, 16), :] = pooled.astype(BF)
         pv_ref[pl.ds(at + 32, 16), :] = sooner(pooled, lane16).astype(BF)
 
-    pl.loop(4, 32, unroll=4)(pool)
+    pl.loop(4, 32, unroll=7)(pool)
+    greeting(0)
 
     ready("wmid", "q2", "bmid")
     base2 = over(wmid_ref[...].reshape(144, 32), q2_ref[...])
@@ -279,52 +304,52 @@
 
     lane32 = iota((32, HALF), 1)
 
-    def middle(first_row, count, acc):
-        for r in range(count):
-            m = jnp.maximum(acc[r * 32 : (r + 1) * 32] + b2_ref[...], 0.0)
-            at = pl.multiple_of((first_row + r) * 96, 32)
-            mv_ref[pl.ds(at, 32), :] = later(m, lane32).astype(BF)
-            mv_ref[pl.ds(at + 32, 32), :] = m.astype(BF)
-            mv_ref[pl.ds(at + 64, 32), :] = sooner(m, lane32).astype(BF)
-
-    def eight(q):
-        window = pv_ref[pl.ds(pl.multiple_of(q * 384, 128), 480), :]
-        middle(q * 8, 8, mm(w2_ref[:, :480], window))
-
-    pl.loop(1, 3)(eight)
-
-    ready("wdec", "q3s", "q3m", "bdec", "wout", "bout")
-    taps = [wdec_ref[dr, dt] for dr in range(3) for dt in range(3)]
-    wskip = jnp.concatenate([t[:, 32:] for t in taps], axis=1)
-    wup = jnp.concatenate([t[:, :32] for t in taps], axis=1)
-    w3s_ref[...] = jnp.zeros(w3s_ref.shape, BF)
+    def convolve(q):
+        if q == 4:
+            return mm(w2_ref[0:64, :192], pv_ref[1536:1728, :])
+        return mm(w2_ref[:, :480], pv_ref[q * 384 : q * 384 + 480, :])
+
+    def middle(q, acc):
+        for r in range(2 if q == 4 else 8):
+            m = jnp.maximum(acc[r * 32 : (r + 1) * 32] + b2_ref[...], 0.0).astype(BF)
+            at = (q * 8 + r + 1) * 224 + 64
+            u_ref[at : at + 32, :] = later(m, lane32)
+            u_ref[at + 32 : at + 64, :] = m
+            u_ref[at + 64 : at + 96, :] = sooner(m, lane32)
+
+    staggered(convolve, middle, (1, 2))
+
+    ready("wdec", "q3", "bdec", "wout", "bout")
+    wdec = jnp.concatenate([wdec_ref[dr, dt] for dr in range(3) for dt in range(3)], axis=1)
     for n in range(4):
-        skip = mm(wskip, q3s_ref[n]).astype(BF)
-        wide = jnp.concatenate([mm(wup, q3m_ref[n]), jnp.zeros((16, 256), F32)], axis=1)
+        wide = jnp.concatenate([mm(wdec, q3_ref[n]), jnp.zeros((16, 640), F32)], axis=1)
         for r in range(4):
-            w3s_ref[pl.ds(r * 64 + n * 16, 16), pl.ds(128 * r, 256)] = skip
-            w3m_ref[pl.ds(r * 64 + n * 16, 16), :] = (
-                pltpu.roll(wide, 96 * r, 1) if r else wide
-            ).astype(BF)
-    b3_ref[...] = column(bdec_ref, 16, HALF)
-    rep = (iota((16, 256), 1) % 16 == iota((16, 256), 0)).astype(F32).astype(BF)
-    wrow = mm(wout_ref[...], rep)
-    orow = iota((16, 256), 0)
-    block = (orow % 8 // 2) * 4 + orow // 8 * 2 + orow % 2
-    wo = jnp.where(iota((16, 256), 1) // 16 == block, wrow, 0.0).astype(BF)
+            turned = pltpu.roll(wide, 224 * r, 1) if r else wide
+            for t in range(10):
+                wf_ref[t, pl.ds(n // 2 * 8 + 2 * r + n % 2, 16, stride=16), :] = (
+                    turned[:, t * 128 : (t + 1) * 128]
+                )
+    w3_ref[...] = jnp.concatenate([wf_ref[t] for t in range(10)], axis=1).astype(BF)
+    wrow = mm(wout_ref[...], jnp.eye(16, dtype=F32).astype(BF))
+    wout = [wrow[:, g : g + 1] for g in range(16)]
     own_ref[...] = mm(clean, split)
     alive_ref[...] = mm(diag, jnp.ones((ROWS, HALF), BF))
 
     forward(1, 0)
 
-    def decode(q):
-        skips = ev_ref[pl.ds(pl.multiple_of(q * 512, 512) + 192, 640), :]
-        mids = mv_ref[pl.ds(pl.multiple_of(q * 384, 128), 576), :]
-        acc = mm(w3s_ref[...], skips) + mm(w3m_ref[:, :576], mids)
-        acc = acc.reshape(16, 16, HALF) + b3_ref[...][None]
-        decoded = jnp.maximum(acc, 0.0).astype(BF).reshape(256, HALF)
-        branch = mm(wo, decoded)
-        here = pl.ds(pl.multiple_of(q * 8, 8), 8)
+    def gather(q):
+        first = q * 896 + 288
+        if not isinstance(q, int):
+            first = pl.multiple_of(first, 32)
+        return mm(w3_ref[:, :1216], u_ref[pl.ds(first, 1216), :])
+
+    def decode(q, acc):
+        branch = None
+        for g in range(16):
+            tile = jnp.maximum(acc[g * 16 : (g + 1) * 16] + bdec_ref[g], 0.0)
+            term = tile.astype(BF).astype(F32) * wout[g]
+            branch = term if branch is None else branch + term
+        here = pl.ds(q * 8 if isinstance(q, int) else pl.multiple_of(q * 8, 8), 8)
         alive = alive_ref[here, :]
         for ps in range(2):
             lanes = slice(ps * HALF, (ps + 1) * HALF)
@@ -355,10 +380,10 @@
             send_sem=x_send.at[1 + h], recv_sem=x_recv.at[1],
             device_id=(zl, c, h), device_id_type=MESH)
 
-    for q in (2, 3):
-        decode(q)
+    staggered(gather, decode, (2, 3, 4))
     forward(1, 1)
-    decode(4)
+    forward(1, 2)
+    greeting(1)
 
     for h in halos:
         h.wait_recv()
@@ -376,34 +401,33 @@
             cut = edges[n][:, h * 128 : (h + 1) * 128]
             cv_ref[h, pl.ds(n, 8, stride=8), :] = cut[:8]
             cv_ref[h, pl.ds(512 + n, 16, stride=8), :] = cut[8:]
-    encode(0)
-    encode(8)
+    staggered(encode, encoded, (0, 8))
 
     @pl.when(c == 0)
     def _():
-        ev_ref[0:256, :] = jnp.zeros((256, HALF), BF)
+        u_ref[0:448, :] = jnp.zeros((448, HALF), BF)
 
     @pl.when(c == NC - 1)
     def _():
-        ev_ref[68 * 64 : 72 * 64, :] = jnp.zeros((256, HALF), BF)
+        u_ref[34 * 224 : 36 * 224, :] = jnp.zeros((448, HALF), BF)
 
     for i in (0, 1, 2, 3, 32, 33, 34, 35):
         pool(i)
 
-    pl.loop(0, 4, step=3)(eight)
-    middle(32, 2, mm(w2_ref[0:64, :192], pv_ref[pl.ds(1536, 192), :]))
+    staggered(convolve, middle, (0, 3, 4))
 
     @pl.when(c == 0)
     def _():
-        mv_ref[0:96, :] = jnp.zeros((96, HALF), BF)
+        u_ref[288:384, :] = jnp.zeros((96, HALF), BF)
 
     @pl.when(c == NC - 1)
     def _():
-        mv_ref[33 * 96 : 34 * 96, :] = jnp.zeros((96, HALF), BF)
-
-    pl.loop(5 * (1 - p), 5 * (1 - p) + 1)(decode)
-    forward(2, 0)
-    pl.loop(5 * (1 - p) + 1, 8 - 6 * p)(decode)
+        u_ref[34 * 224 + 64 : 34 * 224 + 160, :] = jnp.zeros((96, HALF), BF)
+
+    forward(1, 3)
+    greeting(2)
+    theirs = 6 * (1 - p)
+    staggered(gather, decode, (5, theirs, theirs + 1))
     finish(1 - p)
     to_partner.start()
 
@@ -411,8 +435,9 @@
     def _():
         to_previous(1).start()
 
-    forward(2, 1)
-    pl.loop(5 * p, 2 + 6 * p)(decode)
+    forward(2, 0)
+    greeting(3)
+    staggered(gather, decode, (6 * p, 6 * p + 1))
     finish(p)
 
     @pl.when(p == 0)
@@ -420,6 +445,7 @@
         to_previous(0).start()
 
     xw_ref[p] = sd_ref[p]
+    forward(2, 1)
 
     ready("f")
 
@@ -427,7 +453,9 @@
         wide = mm(tg_ref[first : first + count].reshape(count * 128, TL), f_ref[...])
         ts_ref[first : first + count] = wide.reshape(count, 128, 2 * TL)
 
-    transform(0, 5)
+    transform(0, 3)
+    forward(2, 2)
+    greeting(4)
 
     rrow = iota((128, 32), 0)
     repeat = jnp.where(rrow // 4 == iota((128, 32), 1), 1.0, 0.0).astype(BF)
@@ -440,7 +468,8 @@
     z_ref[0] = spectra[0:128] + sign * spectra[128:256]
     z_ref[1] = spectra[128:256]
 
-    forward(3, 0)
+    forward(2, 3)
+    transform(3, 2)
 
     lane512 = iota((8, TL), 1)
 
@@ -464,20 +493,21 @@
         g_ref[at, 0:TL] = jnp.where(lane512 == 0, a, a + b)
         g_ref[at, TL : 2 * TL] = jnp.where(lane512 == 0, b, d)
 
-    pl.loop(0, 5)(functools.partial(product, 0))
-    right(2, 1).wait_recv()
-    left(2, 0).wait_recv()
-    transform(5, 2)
-    pl.loop(5, 7)(functools.partial(product, 0))
+    pl.loop(0, 5, unroll=True)(functools.partial(product, 0))
+    forward(3, 0)
 
     to_previous(0).wait_recv()
     following = xw_ref[2] * jnp.where(z == NZ - 1, 0.0, 1.0).astype(BF)
     z_ref[1] = z_ref[1] + sign * mm(mm(repeat, following).astype(BF), f_ref[...])
-    pl.loop(0, 7)(functools.partial(product, 1))
-    right(3, 0).wait_recv()
-    left(3, 1).wait_recv()
+    pl.loop(0, 5, unroll=True)(functools.partial(product, 1))
+    forward(3, 1)
+    arrived(2, 2, 4)
+    transform(5, 2)
+    pl.loop(5, 7, unroll=True)(functools.partial(product, 0))
+    pl.loop(5, 7, unroll=True)(functools.partial(product, 1))
+    arrived(3, 0, 2)
     transform(7, 1)
-    pl.loop(0, 2)(lambda n: product(n, 7))
+    pl.loop(0, 2, unroll=True)(lambda n: product(n, 7))
 
     ready("i")
     lags = mm(g_ref[...].astype(BF), i_ref[...])
@@ -546,12 +576,10 @@
     results(1).wait()
     for h in halos:
         h.wait_send()
-    for s in range(3):
-        for n in range(2):
+    for s in range(4):
+        for n in range(4 if s < 3 else 2):
             right(s, n).wait_send()
             left(s, n).wait_send()
-    right(3, 0).wait_send()
-    left(3, 1).wait_send()
     to_partner.wait_send()
 
     @pl.when(p == 0)
@@ -568,10 +596,9 @@
     vm = pl.BlockSpec(memory_space=pltpu.VMEM)
     hbm = pl.BlockSpec(memory_space=pltpu.HBM)
     dma = pltpu.SemaphoreType.DMA
-    q3s, q3m = decoder_tables()
     tables = [
         jnp.asarray(t, BF)
-        for t in (encoder_table(), middle_table(), q3s, q3m, spectrum_table(), lag_table())
+        for t in (encoder_table(), middle_table(), decoder_table(), spectrum_table(), lag_table())
     ]
     operands = [
         raw,
@@ -606,16 +633,14 @@
             pltpu.VMEM((2, 640, 128), F32),
             pltpu.VMEM((512, 128), BF),
             pltpu.VMEM((256, 512), BF),
-            pltpu.VMEM((256, 640), BF),
-            pltpu.VMEM((256, 640), BF),
-            pltpu.VMEM((72 * 64, HALF), BF),
+            pltpu.VMEM((10, 256, 128), F32),
+            pltpu.VMEM((256, 1280), BF),
+            pltpu.VMEM((36 * 224, HALF), BF),
             pltpu.VMEM((36 * 48, HALF), BF),
-            pltpu.VMEM((34 * 96, HALF), BF),
             pltpu.VMEM((ROWS, TL), F32),
             pltpu.VMEM((ROWS, TL), F32),
             pltpu.VMEM((ROWS, HALF), F32),
             pltpu.VMEM((32, HALF), F32),
-            pltpu.VMEM((16, HALF), F32),
             pltpu.VMEM((NZ, 128, TL), BF),
             pltpu.VMEM((NZ, 128, 2 * TL), F32),
             pltpu.VMEM((2, 32, TL), BF),
@@ -632,14 +657,15 @@
             dma((2,)),
             dma((2,)),
             dma((2,)),
-            dma((2, 8)),
-            dma((2, 8)),
+            dma((2, 14)),
+            dma((2, 14)),
             dma((3,)),
             dma((2,)),
             dma((1,)),
             dma((1,)),
             dma((NZ,)),
             dma((NZ,)),
+            pltpu.SemaphoreType.REGULAR((5,)),
         ],
         compiler_params=pltpu.CompilerParams(
             collective_id=0, has_side_effects=True, vmem_limit_bytes=56 * 1024 * 1024

time: 43.7 us -> 42.9 us (0.982)
  Pallas kernels: 40.2 us -> 38.6 us
  local copies, waits for them, and re-layouts: 2.09 us -> 2.8 us
    pallas_call x1, Pallas kernels: 40.2 us -> 38.6 us  [body(): pl.pallas_call(kernel, out_shape=(jax.ShapeDtypeStruct((ROWS, TL), BF), j...]
    unnamed x4 -> x2, local copies, waits for them, and re-layouts: 2.09 us -> 2.8 us
where the time goes in v4:
time: 42.9 us; the launch traced here: 42.7 us
  Pallas kernels  38.6 us (90%)
  local copies, waits for them, and re-layouts  2.8 us (7%)
  between operations  1.29 us (3%)
    pallas_call x1, Pallas kernels, body(): pl.pallas_call(kernel, out_shape=(jax.ShapeDtypeStruct((ROWS, TL), BF), j...  38.6 us
    unnamed x2, local copies, waits for them, and re-layouts  2.8 us

profile of v4, /device:TPU:1, one launch (start us, length us, event | category | flops | bytes accessed | tf_op | source)
XLA Modules:
  0.0 42.7 jit_solution(15560469453143270597)
XLA Ops:
  1.3 38.6 %shard_map.176 = (bf16[64,512]{1,0:T(8,128)(2,1)}, f32[4,8,1,32]{3,2,1,0:T(1,128)}) custom-call(bf16[64,512]{1,0:T(8,128)(2,1)} %raw_hbm.1, s32[1,64]{1,0:T(1,128)} %bitcast.10, bf16[4,64,512]{2,1,0:T(8,128)(2,1)} %tmpl_hbm.1, s32[4]{0:T(128)} %assign_hbm.1, bf16[3,3,16]{2,1,0:T(4,128)(2,1)} %bitcast.9, f32[16]{0:T(128)} %benc_hbm.1, ...), custom_call_target="tpu_custom_call" | custom-call | tf_op jit(solution)/shard_map/pallas_call | solution.py:622
  39.9 1.5 %copy.22 = bf16[64,512]{1,0:T(8,128)(2,1)} copy(bf16[64,512]{1,0:T(8,128)(2,1)} %get-tuple-element.4) | data formatting | bytes 131072
  41.4 1.3 %copy.23 = f32[4,8,1,32]{3,2,1,0:T(1,128)} copy(f32[4,8,1,32]{3,2,1,0:T(1,128)} %get-tuple-element.5) | data formatting | bytes 8192

commit v5 on v4

--- a/solution.py
+++ b/solution.py
@@ -186,22 +186,27 @@
 
     def right(s, n):
         part = pl.ds(n * 32, 32)
+        source, target, hops = (3, 7, 2) if s == 3 else (max(2 * s - 1, 0), 2 * s + 1, 1)
         return pltpu.make_async_remote_copy(
-            src_ref=tg_ref.at[max(2 * s - 1, 0), part], dst_ref=tg_ref.at[2 * s + 1, part],
+            src_ref=tg_ref.at[source, part], dst_ref=tg_ref.at[target, part],
             send_sem=ring_send.at[0, 4 * s + n], recv_sem=ring_recv.at[0, 4 * s + n],
-            device_id=(zr, c, p), device_id_type=MESH)
+            device_id=(lax.rem(z + hops, NZ), c, p), device_id_type=MESH)
 
     def left(s, n):
         part = pl.ds(96 - n * 32, 32)
+        source, target, hops = (4, 7, 2) if s == 3 else (2 * s, 2 * s + 2, 1)
         return pltpu.make_async_remote_copy(
-            src_ref=tg_ref.at[2 * s, part], dst_ref=tg_ref.at[min(2 * s + 2, 7), part],
+            src_ref=tg_ref.at[source, part], dst_ref=tg_ref.at[target, part],
             send_sem=ring_send.at[1, 4 * s + n], recv_sem=ring_recv.at[1, 4 * s + n],
-            device_id=(zl, c, p), device_id_type=MESH)
+            device_id=(lax.rem(z + NZ - hops, NZ), c, p), device_id_type=MESH)
 
     def forward(s, n):
         right(s - 1, n).wait_recv()
+        left(s - 1, n).wait_recv()
+        if s == 2 and n < 2:
+            right(3, n).start()
+            left(3, n).start()
         right(s, n).start()
-        left(s - 1, n).wait_recv()
         left(s, n).start()
 
     def arrived(s, first, last):
@@ -318,6 +323,8 @@
             u_ref[at + 64 : at + 96, :] = sooner(m, lane32)
 
     staggered(convolve, middle, (1, 2))
+    forward(1, 0)
+    forward(1, 1)
 
     ready("wdec", "q3", "bdec", "wout", "bout")
     wdec = jnp.concatenate([wdec_ref[dr, dt] for dr in range(3) for dt in range(3)], axis=1)
@@ -335,7 +342,8 @@
     own_ref[...] = mm(clean, split)
     alive_ref[...] = mm(diag, jnp.ones((ROWS, HALF), BF))
 
-    forward(1, 0)
+    forward(1, 2)
+    forward(1, 3)
 
     def gather(q):
         first = q * 896 + 288
@@ -381,8 +389,6 @@
             device_id=(zl, c, h), device_id_type=MESH)
 
     staggered(gather, decode, (2, 3, 4))
-    forward(1, 1)
-    forward(1, 2)
     greeting(1)
 
     for h in halos:
@@ -414,6 +420,7 @@
     for i in (0, 1, 2, 3, 32, 33, 34, 35):
         pool(i)
 
+    forward(2, 0)
     staggered(convolve, middle, (0, 3, 4))
 
     @pl.when(c == 0)
@@ -424,7 +431,7 @@
     def _():
         u_ref[34 * 224 + 64 : 34 * 224 + 160, :] = jnp.zeros((96, HALF), BF)
 
-    forward(1, 3)
+    forward(2, 1)
     greeting(2)
     theirs = 6 * (1 - p)
     staggered(gather, decode, (5, theirs, theirs + 1))
@@ -435,7 +442,8 @@
     def _():
         to_previous(1).start()
 
-    forward(2, 0)
+    forward(2, 2)
+    forward(2, 3)
     greeting(3)
     staggered(gather, decode, (6 * p, 6 * p + 1))
     finish(p)
@@ -445,7 +453,6 @@
         to_previous(0).start()
 
     xw_ref[p] = sd_ref[p]
-    forward(2, 1)
 
     ready("f")
 
@@ -454,7 +461,6 @@
         ts_ref[first : first + count] = wide.reshape(count, 128, 2 * TL)
 
     transform(0, 3)
-    forward(2, 2)
     greeting(4)
 
     rrow = iota((128, 32), 0)
@@ -468,7 +474,6 @@
     z_ref[0] = spectra[0:128] + sign * spectra[128:256]
     z_ref[1] = spectra[128:256]
 
-    forward(2, 3)
     transform(3, 2)
 
     lane512 = iota((8, TL), 1)
@@ -494,14 +499,11 @@
         g_ref[at, TL : 2 * TL] = jnp.where(lane512 == 0, b, d)
 
     pl.loop(0, 5, unroll=True)(functools.partial(product, 0))
-    forward(3, 0)
-
     to_previous(0).wait_recv()
     following = xw_ref[2] * jnp.where(z == NZ - 1, 0.0, 1.0).astype(BF)
     z_ref[1] = z_ref[1] + sign * mm(mm(repeat, following).astype(BF), f_ref[...])
     pl.loop(0, 5, unroll=True)(functools.partial(product, 1))
-    forward(3, 1)
-    arrived(2, 2, 4)
+    arrived(2, 0, 4)
     transform(5, 2)
     pl.loop(5, 7, unroll=True)(functools.partial(product, 0))
     pl.loop(5, 7, unroll=True)(functools.partial(product, 1))
@@ -526,8 +528,9 @@
                     piece = jnp.where(lane8 == k, moved, piece)
                 rs_ref[n * NC + t * 4 + o] = piece
 
-    @pl.loop(1, 2 * NC)
-    def _(d):
+    hops = [0, 2, 1, 1]
+    steps = [0, 1, 2, 1]
+    for d in sorted(range(1, 2 * NC), key=lambda d: -hops[d // 8] - steps[d // 2 % 4]):
         other = lax.rem(me + d, 2 * NC)
         pltpu.make_async_remote_copy(
             src_ref=rs_ref.at[other], dst_ref=rr_ref.at[d - 1],
@@ -544,7 +547,7 @@
     as_ref[...] = parts[0].reshape(8, 1, 128)
 
     places = [0, 1, -1, 2, -2, 3, -3, 4]
-    for d in range(1, NZ):
+    for d in range(NZ - 1, 0, -1):
         pltpu.make_async_remote_copy(
             src_ref=as_ref.at[d], dst_ref=ar_ref.at[z],
             send_sem=a_send.at[d], recv_sem=a_recv.at[z],

time: 42.9 us -> 42.1 us (0.981)
  Pallas kernels: 38.6 us -> 37.8 us
    pallas_call x1, Pallas kernels: 38.6 us -> 37.8 us  [body(): pl.pallas_call(kernel, out_shape=(jax.ShapeDtypeStruct((ROWS, TL), BF), j...]
where the time goes in v5:
time: 42.1 us; the launch traced here: 41.9 us
  Pallas kernels  37.8 us (90%)
  local copies, waits for them, and re-layouts  2.8 us (7%)
  between operations  1.29 us (3%)
    pallas_call x1, Pallas kernels, body(): pl.pallas_call(kernel, out_shape=(jax.ShapeDtypeStruct((ROWS, TL), BF), j...  37.8 us
    unnamed x2, local copies, waits for them, and re-layouts  2.8 us

profile of v5, /device:TPU:1, one launch (start us, length us, event | category | flops | bytes accessed | tf_op | source)
XLA Modules:
  0.0 41.9 jit_solution(9342146263907199102)
XLA Ops:
  1.3 37.8 %shard_map.176 = (bf16[64,512]{1,0:T(8,128)(2,1)}, f32[4,8,1,32]{3,2,1,0:T(1,128)}) custom-call(bf16[64,512]{1,0:T(8,128)(2,1)} %raw_hbm.1, s32[1,64]{1,0:T(1,128)} %bitcast.10, bf16[4,64,512]{2,1,0:T(8,128)(2,1)} %tmpl_hbm.1, s32[4]{0:T(128)} %assign_hbm.1, bf16[3,3,16]{2,1,0:T(4,128)(2,1)} %bitcast.9, f32[16]{0:T(128)} %benc_hbm.1, ...), custom_call_target="tpu_custom_call" | custom-call | tf_op jit(solution)/shard_map/pallas_call | solution.py:625
  39.1 1.5 %copy.22 = bf16[64,512]{1,0:T(8,128)(2,1)} copy(bf16[64,512]{1,0:T(8,128)(2,1)} %get-tuple-element.4) | data formatting | bytes 131072
  40.6 1.3 %copy.23 = f32[4,8,1,32]{3,2,1,0:T(1,128)} copy(f32[4,8,1,32]{3,2,1,0:T(1,128)} %get-tuple-element.5) | data formatting | bytes 8192

commit v6 on v5

--- a/solution.py
+++ b/solution.py
@@ -181,9 +181,6 @@
             send_sem=halo_send.at[1], recv_sem=halo_recv.at[1],
             device_id=(z, down, p), device_id_type=MESH),
     ]
-    for h in halos:
-        h.start()
-
     def right(s, n):
         part = pl.ds(n * 32, 32)
         source, target, hops = (3, 7, 2) if s == 3 else (max(2 * s - 1, 0), 2 * s + 1, 1)
@@ -214,7 +211,12 @@
             right(s, n).wait_recv()
             left(s, n).wait_recv()
 
-    for n in range(4):
+    for n in range(2):
+        right(0, n).start()
+        left(0, n).start()
+    for h in halos:
+        h.start()
+    for n in range(2, 4):
         right(0, n).start()
         left(0, n).start()
 
@@ -504,12 +506,10 @@
     z_ref[1] = z_ref[1] + sign * mm(mm(repeat, following).astype(BF), f_ref[...])
     pl.loop(0, 5, unroll=True)(functools.partial(product, 1))
     arrived(2, 0, 4)
-    transform(5, 2)
-    pl.loop(5, 7, unroll=True)(functools.partial(product, 0))
-    pl.loop(5, 7, unroll=True)(functools.partial(product, 1))
     arrived(3, 0, 2)
-    transform(7, 1)
-    pl.loop(0, 2, unroll=True)(lambda n: product(n, 7))
+    transform(5, 3)
+    pl.loop(5, 8, unroll=True)(functools.partial(product, 0))
+    pl.loop(5, 8, unroll=True)(functools.partial(product, 1))
 
     ready("i")
     lags = mm(g_ref[...].astype(BF), i_ref[...])

time: 42.1 us -> 41.9 us (level)
  no operation moved by 1% of the time
where the time goes in v6:
time: 41.9 us; the launch traced here: 41.7 us
  Pallas kernels  37.7 us (90%)
  local copies, waits for them, and re-layouts  2.8 us (7%)
  between operations  1.29 us (3%)
    pallas_call x1, Pallas kernels, body(): pl.pallas_call(kernel, out_shape=(jax.ShapeDtypeStruct((ROWS, TL), BF), j...  37.7 us
    unnamed x2, local copies, waits for them, and re-layouts  2.8 us

profile of v6, /device:TPU:1, one launch (start us, length us, event | category | flops | bytes accessed | tf_op | source)
XLA Modules:
  0.0 41.7 jit_solution(10720675574835322181)
XLA Ops:
  1.3 37.7 %shard_map.176 = (bf16[64,512]{1,0:T(8,128)(2,1)}, f32[4,8,1,32]{3,2,1,0:T(1,128)}) custom-call(bf16[64,512]{1,0:T(8,128)(2,1)} %raw_hbm.1, s32[1,64]{1,0:T(1,128)} %bitcast.10, bf16[4,64,512]{2,1,0:T(8,128)(2,1)} %tmpl_hbm.1, s32[4]{0:T(128)} %assign_hbm.1, bf16[3,3,16]{2,1,0:T(4,128)(2,1)} %bitcast.9, f32[16]{0:T(128)} %benc_hbm.1, ...), custom_call_target="tpu_custom_call" | custom-call | tf_op jit(solution)/shard_map/pallas_call | solution.py:625
  38.9 1.5 %copy.22 = bf16[64,512]{1,0:T(8,128)(2,1)} copy(bf16[64,512]{1,0:T(8,128)(2,1)} %get-tuple-element.4) | data formatting | bytes 131072
  40.4 1.3 %copy.23 = f32[4,8,1,32]{3,2,1,0:T(1,128)} copy(f32[4,8,1,32]{3,2,1,0:T(1,128)} %get-tuple-element.5) | data formatting | bytes 8192

commit v7 on v6

--- a/solution.py
+++ b/solution.py
@@ -140,8 +140,11 @@
     barrier = pltpu.get_barrier_semaphore()
     up = lax.rem(c + NC - 1, NC)
     down = lax.rem(c + 1, NC)
-    flip = lambda n: c + n - 2 * n * lax.rem(c // n, 2)
-    partners = [(z, flip(n), p) for n in (1, 2, 4, 8)] + [(z, c, 1 - p)]
+    flip = lambda n: n - 2 * n * lax.rem(c // n, 2)
+    partners = [
+        (z, c + flip(1), p), (z, c + flip(2), p), (z, c + flip(2) + flip(4), p),
+        (z, c, 1 - p), (z, c + flip(8), 1 - p),
+    ]
     greeted = partners[1:] + [
         (z, up, p), (z, down, p), (zr, c, p), (zl, c, p), (zr, c, 1 - p), (zl, c, 1 - p)
     ]

time: 41.9 us -> 41.9 us (level)
  no operation moved by 1% of the time
where the time goes in v7:
time: 41.9 us; the launch traced here: 41.7 us
  Pallas kernels  37.7 us (90%)
  local copies, waits for them, and re-layouts  2.8 us (7%)
  between operations  1.29 us (3%)
    pallas_call x1, Pallas kernels, body(): pl.pallas_call(kernel, out_shape=(jax.ShapeDtypeStruct((ROWS, TL), BF), j...  37.7 us
    unnamed x2, local copies, waits for them, and re-layouts  2.8 us

profile of v7, /device:TPU:1, one launch (start us, length us, event | category | flops | bytes accessed | tf_op | source)
XLA Modules:
  0.0 41.7 jit_solution(14607350083112501992)
XLA Ops:
  1.3 37.7 %shard_map.176 = (bf16[64,512]{1,0:T(8,128)(2,1)}, f32[4,8,1,32]{3,2,1,0:T(1,128)}) custom-call(bf16[64,512]{1,0:T(8,128)(2,1)} %raw_hbm.1, s32[1,64]{1,0:T(1,128)} %bitcast.10, bf16[4,64,512]{2,1,0:T(8,128)(2,1)} %tmpl_hbm.1, s32[4]{0:T(128)} %assign_hbm.1, bf16[3,3,16]{2,1,0:T(4,128)(2,1)} %bitcast.9, f32[16]{0:T(128)} %benc_hbm.1, ...), custom_call_target="tpu_custom_call" | custom-call | tf_op jit(solution)/shard_map/pallas_call | solution.py:628
  38.9 1.5 %copy.22 = bf16[64,512]{1,0:T(8,128)(2,1)} copy(bf16[64,512]{1,0:T(8,128)(2,1)} %get-tuple-element.4) | data formatting | bytes 131072
  40.4 1.3 %copy.23 = f32[4,8,1,32]{3,2,1,0:T(1,128)} copy(f32[4,8,1,32]{3,2,1,0:T(1,128)} %get-tuple-element.5) | data formatting | bytes 8192
